TPU v7x, 256 devices: a whole 4x4x8 slice. The times are simulated.
256 devices in a mesh: rep: 16 (over z, core), fsdp: 16 (over x, y).
Axes of the slice: x: 4, y: 4, z: 8, core: 2. Of those that a mesh axis runs over, the one named last changes fastest.
Arguments:
- tokens: bfloat16 [512, 128, 8192], P('rep', 'fsdp'), may hold values from -6 to 6
- cotangent: bfloat16 [512, 128, 1024], P('rep', 'fsdp'), may hold values from -6 to 6
- frozen_weight: bfloat16 [8192, 1024], P('fsdp'), may hold values from -0.0625 to 0.0625
- down_factor_table: bfloat16 [32, 64, 8192], P('rep', None, 'fsdp'), may hold values from -0.0625 to 0.0625
- up_factor_table: bfloat16 [32, 64, 1024], P('rep', 'fsdp'), may hold values from -0.09375 to 0.09375
- adapter_of_block: int32 [512], P('rep'), may hold values from 0 to 31, as said below
- block_destination: int32 [512], P('rep'), may hold values from 0 to 511, as said below
- adapter_table_row: int32 [32], replicated, may hold values from 0 to 31, as said below
Outputs:
- values: bfloat16 [512, 128, 1024], P('rep', 'fsdp')
- token_grad: bfloat16 [512, 128, 8192], P('rep', 'fsdp')
- down_gradient: float32 [32, 64, 8192], P('rep', None, 'fsdp')
- up_gradient: float32 [32, 64, 1024], P('rep', 'fsdp')
Inputs may be any that keep to these rules, and one draw needn't show every extreme that they name: A permutation of the 512 blocks: block b moves to place block_destination[b], on replica block_destination[b] // 32. Of the blocks of one replica at most 2 go to any one replica, and in every draw some replica sends exactly 2 blocks to some replica. A permutation of the adapters. Adapter a's factors and gradients are row adapter_table_row[a] of the tables, and replica adapter_table_row[a] // 2 owns them. Every block's adapter is owned by the replica that the block moves to: adapter_table_row[adapter_of_block[b]] // 2 == block_destination[b] // 32.
All inputs are finite; a program needn't handle non-finite values.
Results may differ from a plain program's by a relative error of at most 0.001.
Values may be sent and summed in bfloat16 or wider, within the bound.
A program may use at most 128 MiB of HBM per device.

v0:
```python
import jax
import jax.numpy as jnp
from jax import lax
from jax.sharding import PartitionSpec as P

lowrank_multiplier = 2.0
highest = lax.Precision.HIGHEST


def local(
    tokens,
    cotangent,
    frozen_weight,
    down_factor_table,
    up_factor_table,
    adapter_of_block,
    block_destination,
    adapter_table_row,
):
    local_tile_groups, block_tokens, feature_count = tokens.shape
    value_width = cotangent.shape[2]
    replicas = lax.axis_size("rep")
    capacity = max(2, (local_tile_groups + replicas - 1) // replicas)
    owned_here = down_factor_table.shape[0]
    slot_count = replicas * capacity
    table_size = adapter_table_row.shape[0]
    dest_rep = block_destination // local_tile_groups
    arrival_slot = block_destination % local_tile_groups
    adapter_matches = (
        adapter_of_block[:, None] == jnp.arange(table_size, dtype=jnp.int32)[None, :]
    ).astype(jnp.int32)
    table_row = jnp.sum(adapter_matches * adapter_table_row[None, :], axis=1)
    local_adapter = table_row - dest_rep * owned_here
    rep_hits = (dest_rep[:, None] == jnp.arange(replicas, dtype=jnp.int32)[None, :]).astype(
        jnp.int32
    )
    earlier = jnp.cumsum(rep_hits, axis=0) - rep_hits
    rank_within = jnp.sum(earlier * rep_hits, axis=1)
    send_pos = dest_rep * capacity + rank_within
    slot_match = (send_pos[None, :] == jnp.arange(slot_count, dtype=jnp.int32)[:, None]).astype(
        jnp.int32
    )
    filled = jnp.sum(slot_match, axis=1)
    source_row = jnp.sum(
        slot_match * jnp.arange(local_tile_groups, dtype=jnp.int32)[None, :], axis=1
    )
    target = jnp.where(filled > 0, jnp.sum(slot_match * arrival_slot[None, :], axis=1), -1)
    adapter_label = jnp.sum(slot_match * local_adapter[None, :], axis=1)
    labels = jnp.stack([target, adapter_label], axis=1)
    outgoing = jnp.take(tokens, source_row, axis=0)
    arrived, arrived_labels = (
        lax.all_to_all(outgoing, "rep", split_axis=0, concat_axis=0, tiled=True),
        lax.all_to_all(labels, "rep", split_axis=0, concat_axis=0, tiled=True),
    )
    lookup = (
        arrived_labels[:, 0][None, :] == jnp.arange(local_tile_groups, dtype=jnp.int32)[:, None]
    ).astype(jnp.int32)
    arrival_row = jnp.sum(lookup * jnp.arange(slot_count, dtype=jnp.int32)[None, :], axis=1)
    adapter_here = jnp.sum(lookup * arrived_labels[:, 1][None, :], axis=1)
    shipped_sequence_items = jnp.take(arrived, arrival_row, axis=0)
    selection_mask = (
        adapter_here[:, None] == jnp.arange(owned_here, dtype=jnp.int32)[None, :]
    ).astype(jnp.float32)
    leading_shrink_operand, expanding_operand = (
        lax.all_gather(down_factor_table, "fsdp", axis=2, tiled=True),
        lax.all_gather(up_factor_table, "fsdp", axis=1, tiled=True),
    )
    shrink_real = leading_shrink_operand.astype(jnp.float32)
    expand_real = expanding_operand.astype(jnp.float32)
    reduced_middle = jnp.einsum(
        "svn,pwn->svpw",
        shipped_sequence_items,
        leading_shrink_operand,
        preferred_element_type=jnp.float32,
    )
    adapter_middle = jnp.sum(reduced_middle * selection_mask[:, None, :, None], axis=2)
    middle_under_mask = adapter_middle[:, :, None, :] * selection_mask[:, None, :, None]
    backward_every_row = jnp.einsum(
        "btk,jrk->btjr", cotangent, expanding_operand, preferred_element_type=jnp.float32
    )
    lowrank_derivative_sweep = jnp.sum(
        backward_every_row * selection_mask[:, None, :, None], axis=2
    )
    derivative_behind_filter = (
        lowrank_derivative_sweep[:, :, None, :] * selection_mask[:, None, :, None]
    )
    adapter_values = jnp.einsum("btjr,jrk->btk", middle_under_mask, expand_real, precision=highest)
    adapter_gradient = jnp.einsum(
        "snuk,ukm->snm", derivative_behind_filter, shrink_real, precision=highest
    )
    down_partial = lowrank_multiplier * jnp.einsum(
        "btjr,btd->jrd",
        derivative_behind_filter,
        shipped_sequence_items.astype(jnp.float32),
        precision=highest,
    )
    up_partial = lowrank_multiplier * jnp.einsum(
        "btjr,btk->jrk", middle_under_mask, cotangent.astype(jnp.float32), precision=highest
    )
    flat_tokens = shipped_sequence_items.reshape(-1, feature_count)
    flat_cot = cotangent.reshape(-1, value_width)
    piece = lax.all_gather(frozen_weight, "fsdp", axis=0, tiled=True)
    value_acc = jnp.dot(flat_tokens, piece, preferred_element_type=jnp.float32)
    piece_grad = lax.dot_general(
        flat_cot, piece, (((1,), (1,)), ((), ())), preferred_element_type=jnp.float32
    )
    frozen_values = value_acc.reshape(local_tile_groups, block_tokens, value_width)
    fixed_weights_derivative = piece_grad.reshape(local_tile_groups, block_tokens, feature_count)
    values = (frozen_values + lowrank_multiplier * adapter_values).astype(jnp.bfloat16)
    shipped_derivative = (fixed_weights_derivative + lowrank_multiplier * adapter_gradient).astype(
        jnp.bfloat16
    )
    safe_target = jnp.maximum(arrived_labels[:, 0], 0)
    returning = jnp.take(shipped_derivative, safe_target, axis=0)
    sent_back_result = lax.all_to_all(returning, "rep", split_axis=0, concat_axis=0, tiled=True)
    token_grad = jnp.take(sent_back_result, send_pos, axis=0)
    down_gradient_total, up_gradient_total = lax.psum((down_partial, up_partial), "fsdp")
    column_position_index = lax.axis_index("fsdp")
    down_gradient = lax.dynamic_slice_in_dim(
        down_gradient_total,
        column_position_index * down_factor_table.shape[2],
        down_factor_table.shape[2],
        2,
    )
    up_gradient = lax.dynamic_slice_in_dim(
        up_gradient_total,
        column_position_index * up_factor_table.shape[1],
        up_factor_table.shape[1],
        1,
    )
    return (values, token_grad, down_gradient, up_gradient)


def solution(mesh):
    placed = (
        P("rep", "fsdp", None),
        P("rep", "fsdp", None),
        P("fsdp", None),
        P("rep", None, "fsdp"),
        P("rep", "fsdp", None),
        P("rep"),
        P("rep"),
        P(),
    )
    return jax.shard_map(
        local,
        mesh=mesh,
        in_specs=placed,
        out_specs=(
            P("rep", "fsdp", None),
            P("rep", "fsdp", None),
            P("rep", None, "fsdp"),
            P("rep", "fsdp", None),
        ),
        check_vma=False,
    )
```

profile of v0, /device:TPU:1, one launch (start us, length us, event | category | flops | bytes accessed | tf_op | source)
XLA Modules:
  0.0 374.1 jit_solution(11751066827529924641)
XLA Ops:
  7.2 0.0 copy-start
  7.2 0.0 all-gather.3.cloned.1.call-start
  7.2 0.7 all-gather.3.cloned.1.call-update
  7.9 0.9 select_reduce_fusion.3
  8.8 0.7 multiply_subtract_fusion
  9.4 0.1 fusion.46
  9.5 0.1 reduce_window_sum.11
  9.6 0.2 select_reduce_fusion.6
  9.8 0.1 convert_reduce_fusion
  9.9 0.1 stack.7
  10.0 0.1 select_n.42
  10.1 0.6 copy.29
  10.7 10.0 %all-to-all-start.1 = ((s32[16,2,2]{1,2,0:T(2,128)}), s32[16,2,2]{1,2,0:T(2,128)S(1)}, u32[]{:S(2)}, u32[]{:S(2)}) async-start(s32[16,2,2]{1,2,0:T(2,128)} %copy.29), calls=%async_computation.1 | async-start | bytes 32768 | tf_op jit(solution)/shard_map/all_to_all | solution.py:53
  20.7 5.0 %gather_fusion = bf16[32,8,8192]{2,1,0:T(8,128)(2,1)} fusion(bf16[32,8,8192]{2,1,0:T(8,128)(2,1)} %param.10, s32[1024]{0:T(1024)S(1)} %pad_clamp_fusion.3), kind=kCustom, calls=%fused_computation.clone | custom fusion | bytes 8388736 | tf_op jit(solution)/shard_map/jit(_take)/gather | solution.py:50
  25.8 5.2 %broadcast_select_fusion.3 = bf16[32,8,8192]{2,1,0:T(8,128)(2,1)} fusion(bf16[32,8,8192]{2,1,0:T(8,128)(2,1)} %gather_fusion, pred[32]{0:T(512)(128)(4,1)S(1)} %compare_and_fusion.2), kind=kLoop, calls=%fused_computation.20 | loop fusion | flops 2097152 | bytes 8388640 | tf_op jit(solution)/shard_map/jit(_take)/select_n | solution.py:50
  30.9 0.0 all-to-all-done.1
  31.0 7.4 %all-to-all-start = ((bf16[32,8,8192]{2,1,0:T(8,128)(2,1)}), bf16[32,8,8192]{2,1,0:T(8,128)(2,1)}, u32[]{:S(2)}, u32[]{:S(2)}) async-start(bf16[32,8,8192]{2,1,0:T(8,128)(2,1)} %broadcast_select_fusion.3), calls=%async_computation | async-start | bytes 8388608 | tf_op jit(solution)/shard_map/all_to_all | solution.py:52
  38.3 0.0 all-gather.5.cloned.1.call-start
  38.3 0.7 all-gather.5.cloned.1.call-update
  39.1 0.0 copy-done.3
  39.1 20.9 %all_gather.11 = bf16[2,64,1024]{2,0,1:T(2,128)(2,1)S(1)} all-gather(bf16[2,4,1024]{2,0,1:T(2,128)(2,1)S(1)} %copy.31), channel_id=1, replica_groups=mesh['rep'=16,'fsdp'=16] {'fsdp'}, dimensions={1}, use_global_device_ids=true | all-gather | bytes 278528 | tf_op jit(solution)/shard_map/all_gather | solution.py:66
  60.0 0.1 all_to_all.14
  60.1 0.1 select_reduce_fusion
  60.2 0.1 fusion.47
  60.3 0.3 fusion.27
  60.7 70.0 %all-gather.3.cloned.1.call-done = bf16[8192,1024]{1,0:T(8,128)(2,1)} async-done(((bf16[512,1024]{1,0:T(8,128)(2,1)}), bf16[8192,1024]{1,0:T(8,128)(2,1)}) %all-gather.3.cloned.1.call-update) | async-done | bytes 16777232 | tf_op jit(solution)/shard_map/all_gather | solution.py:102
  130.7 19.0 %fusion = f32[32,8,8192]{2,1,0:T(8,128)} fusion(bf16[32,8,1024]{2,1,0:T(8,128)(2,1)S(1)} %copy-done, bf16[8192,1024]{1,0:T(8,128)(2,1)} %all-gather.3.cloned.1.call-done), kind=kOutput, calls=%fused_computation.4 | convolution fusion | flops 4294967296 | bytes 25690112 | tf_op jit(solution)/shard_map/dot_general | solution.py:104
  149.7 35.0 %all-gather.5.cloned.1.call-done = bf16[2,64,8192]{2,1,0:T(8,128)(2,1)} async-done(((bf16[2,64,512]{2,1,0:T(8,128)(2,1)}), bf16[2,64,8192]{2,1,0:T(8,128)(2,1)}) %all-gather.5.cloned.1.call-update) | async-done | bytes 2097168 | tf_op jit(solution)/shard_map/all_gather | solution.py:65
  184.7 8.4 %fusion.6 = bf16[32,8,8192]{2,1,0:T(8,128)(2,1)} fusion(f32[32,8,8192]{2,1,0:T(8,128)} %fusion, bf16[2,64,8192]{2,1,0:T(8,128)(2,1)} %all-gather.5.cloned.1.call-done, f32[32,8,64]{2,1,0:T(8,128)S(1)} %fusion.27, f32[32,2]{1,0:T(8,128)S(1)} %fusion.47), kind=kOutput, calls=%fused_computation.11 | convolution fusion | flops 3227549696 | bytes 14745856 | tf_op jit(solution)/shard_map/snuk,ukm->snm/dot_general | solution.py:88
  193.1 5.0 %gather_fusion.2 = bf16[32,8,8192]{2,1,0:T(8,128)(2,1)} fusion(bf16[32,8,8192]{2,1,0:T(8,128)(2,1)} %fusion.6, s32[1024]{0:T(1024)S(1)} %pad_clamp_fusion.1), kind=kCustom, calls=%fused_computation.2.clone | custom fusion | bytes 8388736 | tf_op jit(solution)/shard_map/jit(_take)/gather | solution.py:114
  198.2 4.7 %broadcast_select_fusion.1 = bf16[32,8,8192]{2,1,0:T(8,128)(2,1)} fusion(bf16[32,8,8192]{2,1,0:T(8,128)(2,1)} %gather_fusion.2, pred[32]{0:T(512)(128)(4,1)S(1)} %broadcast_compare_fusion), kind=kLoop, calls=%fused_computation.18 | loop fusion | flops 2097152 | bytes 8388640 | tf_op jit(solution)/shard_map/jit(_take)/select_n | solution.py:114
  202.9 0.0 all-to-all-done
  202.9 8.6 %all-to-all-start.2 = ((bf16[32,8,8192]{2,1,0:T(8,128)(2,1)}), bf16[32,8,8192]{2,1,0:T(8,128)(2,1)}, u32[]{:S(2)}, u32[]{:S(2)}) async-start(bf16[32,8,8192]{2,1,0:T(8,128)(2,1)} %broadcast_select_fusion.1), calls=%async_computation.2 | async-start | bytes 8388608 | tf_op jit(solution)/shard_map/all_to_all | solution.py:115
  211.4 0.2 all-reduce.3.cloned.1.call-start
  211.7 5.2 %gather_fusion.1 = bf16[32,8,8192]{2,1,0:T(8,128)(2,1)} fusion(bf16[32,8,8192]{2,1,0:T(8,128)(2,1)} %all-to-all-done, s32[1024]{0:T(1024)S(1)} %pad_clamp_fusion.2), kind=kCustom, calls=%fused_computation.1.clone | custom fusion | bytes 8388736 | tf_op jit(solution)/shard_map/jit(_take)/gather | solution.py:60
  216.9 0.0 copy-done.2
  216.9 3.6 fusion.22
  220.5 1.3 fusion.16
  221.8 4.2 %fusion.7 = f32[2,64,8192]{2,1,0:T(8,128)} fusion(f32[32,8,64]{2,1,0:T(8,128)S(1)} %fusion.27, f32[32,2]{1,0:T(8,128)S(1)} %fusion.47, bf16[32,8,8192]{2,1,0:T(8,128)(2,1)S(1)} %copy-done.1, pred[32]{0:T(512)(128)(4,1)S(1)} %compare_and_fusion.1), kind=kOutput, calls=%fused_computation.13 | convolution fusion | flops 3224403968 | bytes 8454432 | tf_op jit(solution)/shard_map/btjr,btd->jrd/dot_general | solution.py:91
  226.0 0.0 all-reduce.3.cloned.1.call-update
  226.0 117.5 %all-reduce.3.cloned.1.call-done = (f32[2,64,8192]{2,1,0:T(8,128)}, f32[2,64,1024]{2,1,0:T(8,128)}) async-done(((f32[2,64,8192]{2,1,0:T(8,128)}, f32[2,64,1024]{2,1,0:T(8,128)}), (f32[2,64,8192]{2,1,0:T(8,128)}, f32[2,64,1024]{2,1,0:T(8,128)})) %all-reduce.3.cloned.1.call-update) | async-done | bytes 4718608 | tf_op jit(solution)/shard_map/psum | solution.py:117
  343.6 1.5 constant_dynamic-slice_fusion.1
  345.1 1.7 constant_dynamic-slice_fusion
  346.7 9.5 %fusion.2 = f32[32,8,1024]{2,1,0:T(8,128)S(1)} fusion(bf16[8192,1024]{1,0:T(8,128)(2,1)} %all-gather.3.cloned.1.call-done, bf16[32,8,8192]{2,1,0:T(8,128)(2,1)} %gather_fusion.1, pred[32]{0:T(512)(128)(4,1)S(1)} %compare_and_fusion.1), kind=kOutput, calls=%fused_computation.6 | convolution fusion | flops 4297064448 | bytes 22020128 | tf_op jit(solution)/shard_map/dot_general | solution.py:103
  356.3 1.6 fusion.15
  357.8 0.0 all-to-all-done.2
  357.8 5.0 %gather_fusion.3 = bf16[32,8,8192]{2,1,0:T(8,128)(2,1)} fusion(bf16[32,8,8192]{2,1,0:T(8,128)(2,1)} %all-to-all-done.2, s32[1024]{0:T(1024)S(1)} %pad_clamp_fusion), kind=kCustom, calls=%fused_computation.3.clone | custom fusion | bytes 8388736 | tf_op jit(solution)/shard_map/jit(_take)/gather | solution.py:116
  362.9 4.7 %broadcast_select_fusion = bf16[32,8,8192]{2,1,0:T(8,128)(2,1)} fusion(bf16[32,8,8192]{2,1,0:T(8,128)(2,1)} %gather_fusion.3, pred[32]{0:T(512)(128)(4,1)S(1)} %get-tuple-element.13), kind=kLoop, calls=%fused_computation.17 | loop fusion | flops 2097152 | bytes 8388640 | tf_op jit(solution)/shard_map/jit(_take)/select_n | solution.py:116
  (22 shorter events, 0.1 us)
Async XLA Ops:
  7.2 53.1 %copy-start = (bf16[32,8,1024]{2,1,0:T(8,128)(2,1)S(1)}, bf16[32,8,1024]{2,1,0:T(8,128)(2,1)}, u32[]{:S(2)}) copy-start(bf16[32,8,1024]{2,1,0:T(8,128)(2,1)} %param.11) | copy-start | bytes 1572868
  7.2 123.5 %all-gather.3.cloned.1.call-start = ((), (), s32[]{:S(2)}) async-start(), calls=%async_computation.3 | async-start | bytes 17825792 | tf_op jit(solution)/shard_map/all_gather | solution.py:102
  10.7 20.2 %all-to-all-start.1 = ((s32[16,2,2]{1,2,0:T(2,128)}), s32[16,2,2]{1,2,0:T(2,128)S(1)}, u32[]{:S(2)}, u32[]{:S(2)}) async-start(s32[16,2,2]{1,2,0:T(2,128)} %copy.29), calls=%async_computation.1 | async-start | bytes 32768 | tf_op jit(solution)/shard_map/all_to_all | solution.py:53
  30.9 8.1 %copy-start.3 = (bf16[2,4,1024]{2,1,0:T(4,128)(2,1)S(1)}, bf16[2,4,1024]{2,1,0:T(4,128)(2,1)}, u32[]{:S(2)}) copy-start(bf16[2,4,1024]{2,1,0:T(4,128)(2,1)} %param.14) | copy-start | bytes 49156
  31.0 171.9 %all-to-all-start = ((bf16[32,8,8192]{2,1,0:T(8,128)(2,1)}), bf16[32,8,8192]{2,1,0:T(8,128)(2,1)}, u32[]{:S(2)}, u32[]{:S(2)}) async-start(bf16[32,8,8192]{2,1,0:T(8,128)(2,1)} %broadcast_select_fusion.3), calls=%async_computation | async-start | bytes 8388608 | tf_op jit(solution)/shard_map/all_to_all | solution.py:52
  38.3 146.4 %all-gather.5.cloned.1.call-start = ((), (), s32[]{:S(2)}) async-start(), calls=%async_computation.4 | async-start | bytes 2228224 | tf_op jit(solution)/shard_map/all_gather | solution.py:65
  202.9 155.0 %all-to-all-start.2 = ((bf16[32,8,8192]{2,1,0:T(8,128)(2,1)}), bf16[32,8,8192]{2,1,0:T(8,128)(2,1)}, u32[]{:S(2)}, u32[]{:S(2)}) async-start(bf16[32,8,8192]{2,1,0:T(8,128)(2,1)} %broadcast_select_fusion.1), calls=%async_computation.2 | async-start | bytes 8388608 | tf_op jit(solution)/shard_map/all_to_all | solution.py:115
  211.4 132.2 %all-reduce.3.cloned.1.call-start = ((), (), s32[]{:S(2)}) async-start(), calls=%async_computation.5 | async-start | bytes 9437184 | tf_op jit(solution)/shard_map/psum | solution.py:117
  211.7 5.2 %copy-start.2 = (bf16[2,64,8192]{2,1,0:T(8,128)(2,1)S(1)}, bf16[2,64,8192]{2,1,0:T(8,128)(2,1)}, u32[]{:S(2)}) copy-start(bf16[2,64,8192]{2,1,0:T(8,128)(2,1)} %all-gather.5.cloned.1.call-done) | copy-start | bytes 6291460
  216.9 5.0 %copy-start.1 = (bf16[32,8,8192]{2,1,0:T(8,128)(2,1)S(1)}, bf16[32,8,8192]{2,1,0:T(8,128)(2,1)}, u32[]{:S(2)}) copy-start(bf16[32,8,8192]{2,1,0:T(8,128)(2,1)} %gather_fusion.1) | copy-start | bytes 12582916
Sparse Core Ops, SparseCore 0:
  10.4 120.2 all-gather.2
  133.1 51.5 all-gather.4
  226.1 117.4 all-reduce.2
where the time goes:
time: 375 us; the launch traced here: 374 us
  waiting for transfers between devices  224 us (60%)
  matrix products  47.9 us (13%)
  starting transfers between devices  26.2 us (7%)
  local copies, waits for them, and re-layouts  24.3 us (6%)
  blocking collectives  20.9 us (6%)
  other arithmetic  16.8 us (4%)
  between operations  13.9 us (4%)
    psum x1, waiting for transfers between devices, local(): lax.psum((down_partial, up_partial), 'fsdp')  118 us
    all_gather x1, waiting for transfers between devices, local(): piece = lax.all_gather(frozen_weight, 'fsdp', axis=0, tiled=True)  70 us
    all_gather x1, waiting for transfers between devices, local(): lax.all_gather(down_factor_table, 'fsdp', axis=2, tiled=True)  35 us
    all_gather x1, blocking collectives, local(): lax.all_gather(up_factor_table, 'fsdp', axis=1, tiled=True)  20.9 us
    dot_general x1, matrix products, local(): lax.dot_general(flat_cot, piece, (((1,), (1,)), ((), ())), preferred_elem...  19 us
    all_to_all x1, starting transfers between devices, local(): lax.all_to_all(labels, 'rep', split_axis=0, concat_axis=0, tiled=True)  9.98 us
    dot_general x1, matrix products, local(): value_acc = jnp.dot(flat_tokens, piece, preferred_element_type=jnp.float32)  9.53 us
    all_to_all x1, starting transfers between devices, local(): lax.all_to_all(returning, 'rep', split_axis=0, concat_axis=0, tiled=True)  8.57 us
  transfers between devices with their start and end apart: 6, of which 3 were waited for; matrix products, arithmetic and copies ran while one was open for 21% of the time, Pallas kernels for 0%

commit v1 on v0

v1 whole, which is shorter than its diff:
```python
import functools

import jax
import jax.numpy as jnp
import numpy as np
from jax import lax
from jax.experimental import pallas as pl
from jax.experimental.pallas import tpu as pltpu
from jax.sharding import PartitionSpec as P

MESH = pl.DeviceIdType.MESH
bf16, f32 = jnp.bfloat16, jnp.float32

NR = 16
NF = 16
T = 256
RT = T // NR
D = 8192
V = 1024
DS = D // NF
HALF = DS // 2
A = 128
G = 4
GC = D // G

PLANE = [(i % 4, (i + i // 4) % 4) for i in range(1, 16)]
REPS = [(dz, dc) for dz in (4, 3, 5, 2, 6, 1, 7) for dc in (0, 1)] + [(0, 1)]


def nt(a, b):
    return lax.dot_general(a, b, (((1,), (1,)), ((), ())), preferred_element_type=f32)


def nn(a, b):
    return jnp.dot(a, b, preferred_element_type=f32)


def split(v):
    hi = v.astype(bf16)
    return hi, (v - hi.astype(f32)).astype(bf16)


def kernel(
    tok, cot, w, down, up, sel, selt, lab, q,
    tg, val, dg, ug,
    xs, xr, gs, gr, wf, dn, upr, labr, dpart, drecv, upart, urecv, cotp, gcat, gtcat, upb, acc, mid,
    tok_sem, x_send, x_recv, lab_sem, dn_sem, up_sem, w_own, w_send, w_recv, sib_send, sib_recv,
    g_send, g_recv, r_sem, u_sem, out_sem,
):
    rep, fs = lax.axis_index("rep"), lax.axis_index("fsdp")
    z, c, x, y = rep // 2, rep % 2, fs // 4, fs % 4
    plane = [((x + dx) % 4) * 4 + (y + dy) % 4 for dx, dy in PLANE]
    reps = [((z + dz) % 8) * 2 + (c + dc) % 2 for dz, dc in REPS]
    sib = rep + 1 - 2 * c

    barrier = pltpu.get_barrier_semaphore()
    for r in reps:
        pl.semaphore_signal(barrier, inc=1, device_id=(r, fs), device_id_type=MESH)
    for f in plane:
        pl.semaphore_signal(barrier, inc=1, device_id=(rep, f), device_id_type=MESH)

    def group(g):
        return pl.ds(pl.multiple_of(g * GC, GC), GC)

    def loads(g):
        return pltpu.make_async_copy(tok.at[:, group(g)], gs.at[:, group(g)], tok_sem.at[g])

    for g in range(G):
        loads(g).start()
    pl.semaphore_wait(barrier, len(reps) + len(plane))

    def rows(r):
        return pl.ds(pl.multiple_of(r * RT, RT), RT)

    def push(src, dst, send, recv, r, f):
        pltpu.make_async_remote_copy(
            src_ref=src, dst_ref=dst, send_sem=send, recv_sem=recv,
            device_id=(r, f), device_id_type=MESH,
        ).start()

    def done(ref, sem):
        pltpu.make_async_copy(ref, ref, sem).wait()

    for r in reps:
        push(lab.at[rows(r)], labr.at[rows(rep)], lab_sem.at[0], lab_sem.at[1], r, fs)
    pltpu.make_async_copy(lab.at[rows(rep)], labr.at[rows(rep)], lab_sem.at[1]).start()
    mine8 = pl.ds(pl.multiple_of(fs * 8, 8), 8)
    for f in plane:
        push(up, upr.at[mine8], up_sem.at[0], up_sem.at[1], rep, f)
    pltpu.make_async_copy(up, upr.at[mine8], up_sem.at[1]).start()
    for f in plane:
        push(down, dn.at[fs], dn_sem.at[0], dn_sem.at[1], rep, f)
    pltpu.make_async_copy(down, dn.at[fs], dn_sem.at[1]).start()

    def wrows(f, h):
        return pl.ds(pl.multiple_of(f * DS + h * HALF, HALF), HALF)

    my_half = pl.ds(pl.multiple_of(c * HALF, HALF), HALF)
    for f in plane:
        push(w.at[my_half], wf.at[wrows(fs, c)], w_send, w_recv.at[fs], rep, f)
    own_w = pltpu.make_async_copy(w, wf.at[pl.ds(pl.multiple_of(fs * DS, DS), DS)], w_own)
    own_w.start()

    for g in range(G):
        loads(g).wait()
        for k in range(GC // 512):
            cols = pl.ds(g * GC + k * 512, 512)
            xs[:, cols] = nn(sel[...], gs[:, cols]).astype(bf16)
        for r in reps:
            push(xs.at[rows(r), group(g)], xr.at[rows(rep), group(g)], x_send.at[g], x_recv.at[g], r, fs)
        pltpu.make_async_copy(
            xs.at[rows(rep), group(g)], xr.at[rows(rep), group(g)], x_recv.at[g]
        ).start()

    done(labr, lab_sem.at[1])
    cotp[...] = nn(labr[:, :T], cot[...]).astype(bf16)
    done(upr, up_sem.at[1])
    upb[...] = nn(q[...], upr[...].astype(bf16)).astype(bf16)
    mask = labr[:, T:].astype(f32)
    back = 2.0 * nt(cotp[...], upb[...]) * mask
    hi, lo = split(back)
    gcat[:, :A] = hi
    gcat[:, A:] = lo
    hi, lo = split(back.T)
    gtcat[:A, :] = hi
    gtcat[A:, :] = lo
    done(dn, dn_sem.at[1])

    def dcols(f):
        return pl.ds(pl.multiple_of(f * DS, DS), DS)

    def grads(f):
        wv = wf[dcols(f), :]
        dv = dn[f]
        out = nt(cotp[...], wv)
        out = out + nn(gcat[:, :A], dv) + nn(gcat[:, A:], dv)
        gs[:, dcols(f)] = out.astype(bf16)
        for r in reps:
            push(gs.at[rows(r), dcols(f)], gr.at[rows(rep), dcols(f)], g_send.at[f], g_recv.at[f], r, fs)
        pltpu.make_async_copy(
            gs.at[rows(rep), dcols(f)], gr.at[rows(rep), dcols(f)], g_recv.at[f]
        ).start()

    own_w.wait()
    grads(fs)

    def from_offset(i):
        return ((x + 4 - i % 4) % 4) * 4 + (y + 8 - (i + i // 4) % 4) % 4

    def forward_half(i):
        f = from_offset(i)
        done(wf.at[wrows(f, c)], w_recv.at[f])
        push(wf.at[wrows(f, c)], wf.at[wrows(f, c)], sib_send, sib_recv.at[f], sib, fs)

    forward_half(1)

    def step(i, _):
        @pl.when(i < 15)
        def _():
            forward_half(i + 1)

        f = from_offset(i)
        done(wf.at[wrows(f, 1 - c)], sib_recv.at[f])
        grads(f)
        return 0

    lax.fori_loop(1, 16, step, 0)

    acc[...] = jnp.zeros_like(acc)
    mid[...] = jnp.zeros_like(mid)

    def fwd_group(g, _):
        done(xr.at[:, group(g)], x_recv.at[g])

        def fwd(k, _):
            f = g * 4 + (y + k) % 4
            xv = xr[:, dcols(f)]
            part = nn(gtcat[...], xv)
            dpart[f] = part[:A] + part[A:]

            @pl.when(f != fs)
            def _():
                push(dpart.at[f], drecv.at[fs], r_sem.at[0], r_sem.at[1], rep, f)

            @pl.when(f == fs)
            def _():
                pltpu.make_async_copy(dpart.at[f], drecv.at[fs], r_sem.at[1]).start()

            acc[...] += nn(xv, wf[dcols(f), :])
            mid[...] += nt(xv, dn[f])
            return 0

        lax.fori_loop(0, 4, fwd, 0)
        return 0

    lax.fori_loop(0, G, fwd_group, 0)

    m2 = 2.0 * mid[...] * labr[:, T:].astype(f32)
    hi, lo = split(m2)
    out = acc[...] + nn(hi, upb[...]) + nn(lo, upb[...])
    val[...] = lax.dot_general(
        labr[:, :T], out.astype(bf16), (((0,), (0,)), ((), ())), preferred_element_type=f32
    ).astype(bf16)
    hi, lo = split(m2.T)
    hi = lax.dot_general(q[...], hi, (((0,), (0,)), ((), ())), preferred_element_type=f32).astype(bf16)
    lo = lax.dot_general(q[...], lo, (((0,), (0,)), ((), ())), preferred_element_type=f32).astype(bf16)
    upart[...] = nn(hi, cotp[...]) + nn(lo, cotp[...])
    for f in plane:
        its8 = pl.ds(pl.multiple_of(f * 8, 8), 8)
        push(upart.at[its8], urecv.at[fs], u_sem.at[0], u_sem.at[1], rep, f)
    pltpu.make_async_copy(upart.at[mine8], urecv.at[fs], u_sem.at[1]).start()

    for g in range(G):
        done(xs.at[pl.ds(0, T - RT), group(g)], x_send.at[g])

    def finish(i, _):
        f = from_offset(i)
        done(gr.at[:, dcols(f)], g_recv.at[f])
        xs[:, dcols(f)] = nn(selt[...], gr[:, dcols(f)]).astype(bf16)
        pltpu.make_async_copy(xs.at[:, dcols(f)], tg.at[:, dcols(f)], out_sem).start()
        return 0

    lax.fori_loop(0, 16, finish, 0)

    done(urecv, u_sem.at[1])
    ug[...] = jnp.sum(urecv[...], axis=0)
    done(drecv, r_sem.at[1])

    def total(k, _):
        part = pl.ds(pl.multiple_of(k * 8, 8), 8)
        out = drecv[0, part, :]
        for f in range(1, NF):
            out = out + drecv[f, part, :]
        dg[part, :] = out
        return 0

    lax.fori_loop(0, A // 8, total, 0)

    done(tg, out_sem)
    done(lab.at[pl.ds(0, T - RT)], lab_sem.at[0])
    done(upr.at[pl.ds(0, 15 * 8)], up_sem.at[0])
    done(dn.at[pl.ds(0, 15)], dn_sem.at[0])
    done(wf.at[pl.ds(0, 15 * HALF)], w_send)
    done(wf.at[pl.ds(0, 15 * HALF)], sib_send)
    done(dpart.at[pl.ds(0, 15)], r_sem.at[0])
    done(upart.at[pl.ds(0, 15 * 8)], u_sem.at[0])

    def sent(f, _):
        done(gs.at[pl.ds(0, T - RT), dcols(f)], g_send.at[f])
        return 0

    lax.fori_loop(0, 16, sent, 0)


def rank_order():
    order = np.zeros((A, A), np.float32)
    for k in range(A):
        a, r = k // 64, k % 64
        order[k, (r // 4) * 8 + a * 4 + r % 4] = 1.0
    return order


def local(
    tokens,
    cotangent,
    frozen_weight,
    down_factor_table,
    up_factor_table,
    adapter_of_block,
    block_destination,
    adapter_table_row,
):
    blocks = tokens.shape[0]
    steps = jnp.arange(blocks, dtype=jnp.int32)
    wide = jnp.arange(T, dtype=jnp.int32)
    dest_rep = block_destination // blocks
    slot = block_destination % blocks
    row = jnp.sum(
        jnp.where(adapter_of_block[:, None] == steps[None, :], adapter_table_row[None, :], 0), axis=1
    )
    adapter = row - dest_rep * 2
    before = (dest_rep[:, None] == dest_rep[None, :]) & (steps[None, :] < steps[:, None])
    place = dest_rep * 2 + jnp.sum(before.astype(jnp.int32), axis=1)
    hit = place[None, :] == steps[:, None]
    slot_at = jnp.sum(jnp.where(hit, slot[None, :], 0), axis=1)
    adapter_at = jnp.sum(jnp.where(hit, adapter[None, :], 0), axis=1)

    def by_token(v):
        return jnp.broadcast_to(v[:, None], (blocks, 8)).reshape(T)

    code = by_token(place) * 8 + wide % 8
    slot_code = by_token(slot_at) * 8 + wide % 8
    sel = (wide[:, None] == code[None, :]).astype(bf16)
    selt = (code[:, None] == wide[None, :]).astype(bf16)
    lab = jnp.concatenate(
        [
            (slot_code[:, None] == wide[None, :]).astype(bf16),
            (by_token(adapter_at)[:, None] == (wide // 64)[None, :A]).astype(bf16),
        ],
        axis=1,
    )
    q = jnp.asarray(rank_order(), bf16)

    vm = pl.BlockSpec(memory_space=pltpu.VMEM)
    hbm = pl.BlockSpec(memory_space=pl.ANY)
    dma = pltpu.SemaphoreType.DMA
    tg, val, dg, ug = pl.pallas_call(
        kernel,
        out_shape=(
            jax.ShapeDtypeStruct((T, D), bf16),
            jax.ShapeDtypeStruct((T, V), bf16),
            jax.ShapeDtypeStruct((A, DS), f32),
            jax.ShapeDtypeStruct((8, V), f32),
        ),
        in_specs=[hbm, vm, hbm, hbm, hbm, vm, vm, vm, vm],
        out_specs=(hbm, vm, vm, vm),
        scratch_shapes=[
            pltpu.VMEM((T, D), bf16),
            pltpu.VMEM((T, D), bf16),
            pltpu.VMEM((T, D), bf16),
            pltpu.VMEM((T, D), bf16),
            pltpu.VMEM((D, V), bf16),
            pltpu.VMEM((NF, A, DS), bf16),
            pltpu.VMEM((A, V), f32),
            pltpu.VMEM((T, T + A), bf16),
            pltpu.VMEM((NF, A, DS), f32),
            pltpu.VMEM((NF, A, DS), f32),
            pltpu.VMEM((A, V), f32),
            pltpu.VMEM((NF, 8, V), f32),
            pltpu.VMEM((T, V), bf16),
            pltpu.VMEM((T, 2 * A), bf16),
            pltpu.VMEM((2 * A, T), bf16),
            pltpu.VMEM((A, V), bf16),
            pltpu.VMEM((T, V), f32),
            pltpu.VMEM((T, A), f32),
            dma((G,)),
            dma((G,)),
            dma((G,)),
            dma((2,)),
            dma((2,)),
            dma((2,)),
            dma,
            dma,
            dma((NF,)),
            dma,
            dma((NF,)),
            dma((NF,)),
            dma((NF,)),
            dma((2,)),
            dma((2,)),
            dma,
        ],
        compiler_params=pltpu.CompilerParams(
            collective_id=0, has_side_effects=True, vmem_limit_bytes=60 * 1024 * 1024
        ),
        cost_estimate=pl.CostEstimate(
            flops=14 * 10**9, bytes_accessed=12 * 2**20, transcendentals=0
        ),
        name="lora_moves",
    )(
        tokens.reshape(T, D),
        cotangent.reshape(T, V),
        frozen_weight,
        down_factor_table.reshape(A, DS),
        up_factor_table.astype(f32).reshape(8, V),
        sel,
        selt,
        lab,
        q,
    )
    return (
        val.reshape(blocks, 8, V),
        tg.reshape(blocks, 8, D),
        dg.reshape(2, 64, DS),
        ug.reshape(2, 4, V),
    )


def solution(mesh):
    placed = (
        P("rep", "fsdp", None),
        P("rep", "fsdp", None),
        P("fsdp", None),
        P("rep", None, "fsdp"),
        P("rep", "fsdp", None),
        P("rep"),
        P("rep"),
        P(),
    )
    return jax.shard_map(
        local,
        mesh=mesh,
        in_specs=placed,
        out_specs=(
            P("rep", "fsdp", None),
            P("rep", "fsdp", None),
            P("rep", None, "fsdp"),
            P("rep", "fsdp", None),
        ),
        check_vma=False,
    )
```

time: 375 us -> 282 us (0.75)
  Pallas kernels: 0 us -> 267 us
  waiting for transfers between devices: 224 us -> 0 us
  matrix products: 47.9 us -> 0 us
  starting transfers between devices: 26.2 us -> 0 us
  blocking collectives: 20.9 us -> 0 us
  local copies, waits for them, and re-layouts: 24.3 us -> 10.5 us
  other arithmetic: 16.8 us -> 3.51 us
  between operations: 13.9 us -> 0.7 us
    pallas_call x0 -> x1, Pallas kernels: none -> 267 us  [local(): pl.pallas_call(kernel, out_shape=(jax.ShapeDtypeStruct((T, D), bf16), jax...]
    psum x1 -> x0, waiting for transfers between devices: 118 us -> none  [local(): lax.psum((down_partial, up_partial), 'fsdp')]
    all_gather x2 -> x0, waiting for transfers between devices: 105 us -> none  [the longest x1 70 us: local(): piece = lax.all_gather(frozen_weight, 'fsdp', axis=0, tiled=True)]
    dot_general x8 -> x0, matrix products: 47.9 us -> none  [the longest x1 19 us: local(): lax.dot_general(flat_cot, piece, (((1,), (1,)), ((), ())), preferred_elem...]
    all_to_all x3 -> x0, starting transfers between devices: 25.9 us -> none  [the longest x1 9.98 us: local(): lax.all_to_all(labels, 'rep', split_axis=0, concat_axis=0, tiled=True)]
    all_gather x1 -> x0, blocking collectives: 20.9 us -> none  [local(): lax.all_gather(up_factor_table, 'fsdp', axis=1, tiled=True)]
    gather x4 -> x0, local copies, waits for them, and re-layouts: 20.2 us -> none  [the longest x1 5.16 us: local(): shipped_sequence_items = jnp.take(arrived, arrival_row, axis=0)]
    select_n x7 -> x1, other arithmetic: 14.6 us -> 0.01 us  [local(): wide // 64]
  transfers between devices with their start and end apart: 6 -> 0, of which waited for: 3 -> 0; matrix products, arithmetic and copies ran while one was open for 21% -> 0% of each run, Pallas kernels for 0% -> 0%
where the time goes in v1:
time: 282 us
  Pallas kernels  267 us (95%)
  local copies, waits for them, and re-layouts  10.5 us (4%)
  other arithmetic  3.51 us (1%)
    pallas_call x1, Pallas kernels, local(): pl.pallas_call(kernel, out_shape=(jax.ShapeDtypeStruct((T, D), bf16), jax...  267 us
    unnamed x5, local copies, waits for them, and re-layouts  7.25 us

profile of v1, /device:TPU:1, one launch (start us, length us, event | category | flops | bytes accessed | tf_op | source)
XLA Modules:
  0.0 282.0 jit_solution(10215852850489516129)
XLA Ops:
  0.6 0.9 select_reduce_fusion.1
  1.5 0.7 multiply_subtract_fusion
  2.2 0.2 convert_reduce_fusion
  2.4 0.1 select_reduce_fusion.2
  2.5 0.1 broadcast_in_dim.33
  2.6 0.1 mul.34
  2.7 0.1 broadcast_in_dim.30
  2.7 0.1 mul.32
  2.8 0.1 broadcast_in_dim.36
  2.9 0.1 eq.110
  3.0 0.1 broadcast_compare_fusion
  3.1 1.3 reshape.100.up
  4.5 0.1 iota_compare_fusion
  4.6 0.7 add_convert_fusion.lab
  5.3 0.8 fusion.1
  6.0 267.3 %lora_moves.1 = (bf16[256,8192]{1,0:T(8,128)(2,1)}, bf16[256,1024]{1,0:T(8,128)(2,1)}, f32[128,512]{1,0:T(8,128)}, f32[8,1024]{1,0:T(8,128)}) custom-call(bf16[256,8192]{1,0:T(8,128)(2,1)} %bitcast.9, bf16[256,1024]{1,0:T(8,128)(2,1)} %bitcast.10, bf16[512,1024]{1,0:T(8,128)(2,1)} %w.1, bf16[128,512]{1,0:T(8,128)(2,1)} %bitcast.11, f32[8,1024]{1,0:T(8,128)} %reshape.100.up, ...), custom_call_target="tpu_custom_call" | custom-call | flops 14000000000 | bytes 12582912 | tf_op jit(solution)/shard_map/lora_moves/pallas_call | solution.py:307
  273.3 1.4 reshape.98
  274.7 1.9 copy.16
  276.6 0.0 copy-start
  276.6 4.7 %copy.17 = bf16[32,8,8192]{2,1,0:T(8,128)(2,1)} copy(bf16[32,8,8192]{2,1,0:T(8,128)(2,1)} %bitcast.6) | data formatting | bytes 8388608
  281.3 0.0 copy-done
  281.3 0.7 copy.18
  (6 shorter events, 0.0 us)
Async XLA Ops:
  276.6 4.7 %copy-start = (f32[128,512]{1,0:T(8,128)S(1)}, f32[128,512]{1,0:T(8,128)}, u32[]{:S(2)}) copy-start(f32[128,512]{1,0:T(8,128)} %get-tuple-element.10) | copy-start | bytes 786436

commit v2 on v1

v2 whole, which is shorter than its diff:
```python
import functools

import jax
import jax.numpy as jnp
import numpy as np
from jax import lax
from jax.experimental import pallas as pl
from jax.experimental.pallas import tpu as pltpu
from jax.sharding import PartitionSpec as P

MESH = pl.DeviceIdType.MESH
bf16, f32 = jnp.bfloat16, jnp.float32

NR = 16
NF = 16
T = 256
RT = T // NR
D = 8192
V = 1024
DS = D // NF
HALF = DS // 2
QUARTER = HALF // 2
A = 128
G = 4
GC = D // G

REPS = [(dz, dc) for dz in (4, 3, 5, 2, 6, 1, 7) for dc in (0, 1)] + [(0, 1)]
RING = (1, 3, 2)
FAR = T // 2


def nt(a, b):
    return lax.dot_general(a, b, (((1,), (1,)), ((), ())), preferred_element_type=f32)


def tn(a, b):
    return lax.dot_general(a, b, (((0,), (0,)), ((), ())), preferred_element_type=f32)


def nn(a, b):
    return jnp.dot(a, b, preferred_element_type=f32)


def split(v):
    hi = v.astype(bf16)
    return hi, (v - hi.astype(f32)).astype(bf16)


def arrival_group(dz, dc, c):
    behind = -dz % 8
    if behind in (2, 6):
        return 6 + c * 9 if behind == 2 else 7 + c * 7
    return {0: 0, 1: 2, 7: 4, 4: 8, 5: 10, 3: 12}[behind] + dc


def kernel(
    tok, cot, w, down, up, sel, selt, lab, q,
    tg, val, dg, ug,
    xs, xr, gs, gr, wf, dn, upr, labr, dpart, ra, rb, sa, sb, ra2, rb2, upart, urecv,
    cotp, hc, gcat, hg, gtcat, upb, acc, mid,
    tok_sem, x_send, x_recv, lab_sem, hop_sem, hop_own, up_sem, dn_send, dn_recv, w_own, w_send, w_recv,
    sib_send, sib_recv, far_sem, g_send, g_recv, r_sem, r2_sem, u_sem, out_sem,
):
    rep, fs = lax.axis_index("rep"), lax.axis_index("fsdp")
    z, c, x, y = rep // 2, rep % 2, fs // 4, fs % 4
    plane = [((x + dx) % 4) * 4 + (y + dy) % 4 for dx in range(4) for dy in range(4)][1:]
    reps = [((z + dz) % 8) * 2 + (c + dc) % 2 for dz, dc in REPS]
    sib = rep + 1 - 2 * c
    opposite = ((z + 4) % 8) * 2 + c
    at_x = [((x + d) % 4) * 4 + y for d in RING]
    at_y = [x * 4 + (y + d) % 4 for d in RING]

    barrier = pltpu.get_barrier_semaphore()
    for r in reps:
        pl.semaphore_signal(barrier, inc=1, device_id=(r, fs), device_id_type=MESH)
    for f in plane:
        pl.semaphore_signal(barrier, inc=1, device_id=(rep, f), device_id_type=MESH)

    def group(g):
        return pl.ds(pl.multiple_of(g * GC, GC), GC)

    def loads(g):
        return pltpu.make_async_copy(tok.at[:, group(g)], gs.at[:, group(g)], tok_sem.at[g])

    for g in range(G):
        loads(g).start()
    own_w = pltpu.make_async_copy(w, wf.at[pl.ds(pl.multiple_of(fs * DS, DS), DS)], w_own)
    own_w.start()
    own_down = pltpu.make_async_copy(down, dn.at[fs, :, pl.ds(0, 64), :], hop_own)
    own_down.start()
    mine8 = pl.ds(pl.multiple_of(fs * 8, 8), 8)
    pltpu.make_async_copy(up, upr.at[mine8], up_sem.at[1]).start()
    pl.semaphore_wait(barrier, len(reps) + len(plane))

    def rows(r):
        return pl.ds(pl.multiple_of(r * RT, RT), RT)

    def push(src, dst, send, recv, r, f):
        pltpu.make_async_remote_copy(
            src_ref=src, dst_ref=dst, send_sem=send, recv_sem=recv,
            device_id=(r, f), device_id_type=MESH,
        ).start()

    def done(ref, sem):
        pltpu.make_async_copy(ref, ref, sem).wait()

    for (dz, dc), r in zip(REPS, reps):
        push(lab.at[rows(r)], labr.at[rows(arrival_group(dz, dc, c))], lab_sem.at[0], lab_sem.at[1], r, fs)
    pltpu.make_async_copy(lab.at[rows(rep)], labr.at[pl.ds(0, RT)], lab_sem.at[1]).start()
    push(down, dn.at[fs, :, pl.ds(64, 64), :], hop_sem.at[0], hop_sem.at[1], opposite, fs)
    for f in plane:
        push(up, upr.at[mine8], up_sem.at[0], up_sem.at[1], rep, f)

    def wpart(f, h, core):
        return wf.at[pl.ds(pl.multiple_of(f * DS + core * HALF + h * QUARTER, QUARTER), QUARTER)]

    def push_w(f, h, to):
        push(wpart(f, h, c), wpart(f, h, c), w_send, w_recv.at[f, h], rep, to)

    def push_dn(f, h, to):
        push(dn.at[f, h], dn.at[f, h], dn_send, dn_recv.at[f, h], rep, to)

    own_w.wait()
    for k in range(3):
        push_w(fs, 0, at_x[k])
        push_w(fs, 1, at_y[k])
    for k in range(3):
        push_w(fs, 0, at_y[k])
        push_w(fs, 1, at_x[k])

    def tokens_off(g):
        loads(g).wait()
        for k in range(GC // 512):
            cols = pl.ds(g * GC + k * 512, 512)
            xs[:, cols] = nn(sel[...], gs[:, cols]).astype(bf16)
        for (dz, dc), r in zip(REPS, reps):
            push(
                xs.at[rows(r), group(g)], xr.at[rows(arrival_group(dz, dc, c)), group(g)],
                x_send.at[g], x_recv.at[g], r, fs,
            )
        pltpu.make_async_copy(
            xs.at[rows(rep), group(g)], xr.at[pl.ds(0, RT), group(g)], x_recv.at[g]
        ).start()

    tokens_off(0)

    done(labr, lab_sem.at[1])
    cotp[...] = nn(labr[:, :T], cot[...]).astype(bf16)
    done(upr, up_sem.at[1])
    upb[...] = nn(q[...], upr[...].astype(bf16)).astype(bf16)
    lane = lax.broadcasted_iota(jnp.int32, (T, 2 * A), 1)
    row = lax.broadcasted_iota(jnp.int32, (T, 2 * A), 0)
    second = (lane % A) >= 64
    mask = labr[:, T:].astype(f32)
    back = jnp.where(second == (row >= FAR), 2.0 * nt(cotp[...], upb[...]) * mask, 0.0)
    hi, lo = split(back)
    gcat[:, : 2 * A] = hi
    gcat[:, 2 * A :] = lo
    far = pl.ds(FAR, FAR)
    push(cotp.at[far], hc.at[far], far_sem.at[0], far_sem.at[1], opposite, fs)
    push(gcat.at[far], hg.at[far], far_sem.at[2], far_sem.at[3], opposite, fs)
    hc[:FAR, :] = cotp[:FAR, :]
    hg[:FAR, :] = gcat[:FAR, :]
    own_down.wait()
    done(dn.at[0, :, pl.ds(0, 64), :], hop_sem.at[1])
    for k in range(3):
        push_dn(fs, 0, at_x[k])
        push_dn(fs, 1, at_y[k])
    for k in range(3):
        push_dn(fs, 0, at_y[k])
        push_dn(fs, 1, at_x[k])
    backt = back.T
    folded = jnp.concatenate(
        [backt[0:64] + backt[64:128], backt[128:192] + backt[192:256]], axis=0
    )
    hi, lo = split(folded)
    gtcat[:A, :] = hi
    gtcat[A:, :] = lo

    tokens_off(1)

    for k in range(3):
        fx, fy = ((x + 4 - RING[k]) % 4) * 4 + y, x * 4 + (y + 4 - RING[k]) % 4
        done(wpart(fx, 0, c), w_recv.at[fx, 0])
        done(wpart(fy, 1, c), w_recv.at[fy, 1])
        for j in range(3):
            push_w(fx, 0, at_y[j])
            push_w(fy, 1, at_x[j])
    tokens_off(2)
    for k in range(3):
        fx, fy = ((x + 4 - RING[k]) % 4) * 4 + y, x * 4 + (y + 4 - RING[k]) % 4
        done(dn.at[fx, 0], dn_recv.at[fx, 0])
        done(dn.at[fy, 1], dn_recv.at[fy, 1])
        for j in range(3):
            push_dn(fx, 0, at_y[j])
            push_dn(fy, 1, at_x[j])
    tokens_off(3)
    done(hc.at[far], far_sem.at[1])
    done(hg.at[far], far_sem.at[3])

    def dcols(f):
        return pl.ds(pl.multiple_of(f * DS, DS), DS)

    owner, other = rep, opposite
    back_to = []
    for dz, base in ((0, 0), (1, 2), (7, 4)):
        for dc in (0, 1):
            back_to.append((base + dc, ((z + dz) % 8) * 2 + (c + dc) % 2, owner))
            back_to.append((8 + base + dc, ((z + dz) % 8) * 2 + (c + dc) % 2, other))
    for k, dz in ((6, 2), (7, 6)):
        back_to.append((k, ((z + dz) % 8) * 2, owner))
        back_to.append((8 + k, ((z + dz) % 8) * 2 + 1, other))
    remote = [e for e in back_to if e[0] not in (0, 8)]
    remote = remote[-4:] + remote[:-4]

    def grads(f):
        dv = dn[f].reshape(2 * A, DS)
        out = nt(hc[...], wf[dcols(f), :])
        out = out + nn(hg[:, : 2 * A], dv) + nn(hg[:, 2 * A :], dv)
        gs[:, dcols(f)] = out.astype(bf16)
        for k, r, place in remote:
            push(
                gs.at[pl.ds(k * RT, RT), dcols(f)], gr.at[rows(place), dcols(f)],
                g_send.at[f], g_recv.at[f], r, fs,
            )
        for k, place in ((0, owner), (8, other)):
            pltpu.make_async_copy(
                gs.at[pl.ds(k * RT, RT), dcols(f)], gr.at[rows(place), dcols(f)], g_recv.at[f]
            ).start()

    grads(fs)

    def from_offset(i):
        return ((x + 4 - i % 4) % 4) * 4 + (y + 4 - i // 4) % 4

    def whalf(f, core):
        return wf.at[pl.ds(pl.multiple_of(f * DS + core * HALF, HALF), HALF)]

    def half_in(i):
        f = from_offset(i)
        @pl.when(i // 4 != 0)
        def _():
            done(wpart(f, 0, c), w_recv.at[f, 0])
            done(dn.at[f, 0], dn_recv.at[f, 0])

        @pl.when(i % 4 != 0)
        def _():
            done(wpart(f, 1, c), w_recv.at[f, 1])
            done(dn.at[f, 1], dn_recv.at[f, 1])

        push(whalf(f, c), whalf(f, c), sib_send, sib_recv.at[f], sib, fs)

    half_in(1)

    def step(i, _):
        @pl.when(i < 15)
        def _():
            half_in(i + 1)

        f = from_offset(i)
        done(whalf(f, 1 - c), sib_recv.at[f])
        grads(f)
        return 0

    lax.fori_loop(1, 16, step, 0)

    acc[...] = jnp.zeros_like(acc)
    mid[...] = jnp.zeros_like(mid)

    def fwd_group(g, _):
        done(xr.at[:, group(g)], x_recv.at[g])

        def fwd(k, _):
            fy = (y + k) % 4
            f = g * 4 + fy
            xv = xr[:, dcols(f)]
            part = nn(gtcat[...], xv)
            dpart[f] = part[:A] + part[A:]

            @pl.when(g != x)
            def _():
                push(dpart.at[f, pl.ds(0, 64)], ra.at[x, fy], r_sem.at[0], r_sem.at[1], rep, g * 4 + y)

            @pl.when(fy != y)
            def _():
                push(dpart.at[f, pl.ds(64, 64)], rb.at[y, g], r_sem.at[2], r_sem.at[3], rep, x * 4 + fy)

            acc[...] += nn(xv, wf[dcols(f), :])
            mid[...] += nt(xv, dn[f].reshape(2 * A, DS))
            return 0

        lax.fori_loop(0, 4, fwd, 0)
        return 0

    lax.fori_loop(0, G, fwd_group, 0)

    m2 = jnp.where(second, 0.0, 2.0 * mid[...] * mask)
    hi, lo = split(m2)
    out = acc[...] + nn(hi, upb[...]) + nn(lo, upb[...])
    val[...] = tn(labr[:, :T], out.astype(bf16)).astype(bf16)
    hi, lo = split(m2.T)
    hi = tn(q[...], hi).astype(bf16)
    lo = tn(q[...], lo).astype(bf16)
    upart[...] = nn(hi, cotp[...]) + nn(lo, cotp[...])
    for f in plane:
        push(upart.at[pl.ds(pl.multiple_of(f * 8, 8), 8)], urecv.at[fs], u_sem.at[0], u_sem.at[1], rep, f)
    pltpu.make_async_copy(upart.at[mine8], urecv.at[fs], u_sem.at[1]).start()

    done(ra.at[pl.ds(0, 3)], r_sem.at[1])
    done(rb.at[pl.ds(0, 3)], r_sem.at[3])

    def first_sum(k, _):
        own_a, own_b = dpart[x * 4 + k, :64, :], dpart[k * 4 + y, 64:, :]
        for d in RING:
            own_a = own_a + ra[(x + d) % 4, k]
            own_b = own_b + rb[(y + d) % 4, k]
        sa[k] = own_a
        sb[k] = own_b

        @pl.when(k != y)
        def _():
            push(sa.at[k], ra2.at[y], r2_sem.at[0], r2_sem.at[1], rep, x * 4 + k)

        @pl.when(k != x)
        def _():
            push(sb.at[k], rb2.at[x], r2_sem.at[2], r2_sem.at[3], rep, k * 4 + y)

        return 0

    lax.fori_loop(0, 4, first_sum, 0)

    for g in range(G):
        done(xs.at[pl.ds(0, T - RT), group(g)], x_send.at[g])

    def finish(i, _):
        f = from_offset(i)
        done(gr.at[:, dcols(f)], g_recv.at[f])
        xs[:, dcols(f)] = nn(selt[...], gr[:, dcols(f)]).astype(bf16)
        pltpu.make_async_copy(xs.at[:, dcols(f)], tg.at[:, dcols(f)], out_sem).start()
        return 0

    lax.fori_loop(0, 16, finish, 0)

    done(urecv, u_sem.at[1])
    ug[...] = jnp.sum(urecv[...], axis=0)
    done(ra2.at[pl.ds(0, 3)], r2_sem.at[1])
    done(rb2.at[pl.ds(0, 3)], r2_sem.at[3])
    sum_a, sum_b = sa[y], sb[x]
    for d in RING:
        sum_a = sum_a + ra2[(y + d) % 4]
        sum_b = sum_b + rb2[(x + d) % 4]
    dg[:64, :] = sum_a
    dg[64:, :] = sum_b

    done(tg, out_sem)
    done(lab.at[pl.ds(0, T - RT)], lab_sem.at[0])
    done(down, hop_sem.at[0])
    done(cotp.at[far], far_sem.at[0])
    done(gcat.at[far], far_sem.at[2])
    done(upr.at[pl.ds(0, 15 * 8)], up_sem.at[0])
    done(dn.at[pl.ds(0, 15)], dn_send)
    done(wf.at[pl.ds(0, 30 * QUARTER)], w_send)
    done(wf.at[pl.ds(0, 15 * HALF)], sib_send)
    done(ra.at[pl.ds(0, 3)], r_sem.at[0])
    done(rb.at[pl.ds(0, 3)], r_sem.at[2])
    done(ra2.at[pl.ds(0, 3)], r2_sem.at[0])
    done(rb2.at[pl.ds(0, 3)], r2_sem.at[2])
    done(upart.at[pl.ds(0, 15 * 8)], u_sem.at[0])

    def sent(f, _):
        done(gs.at[pl.ds(0, 14 * RT), dcols(f)], g_send.at[f])
        return 0

    lax.fori_loop(0, 16, sent, 0)


def rank_order():
    order = np.zeros((2 * A, A), np.float32)
    for k in range(2 * A):
        a, r = k // A, k % 64
        order[k, (r // 4) * 8 + a * 4 + r % 4] = 1.0
    return order


def local(
    tokens,
    cotangent,
    frozen_weight,
    down_factor_table,
    up_factor_table,
    adapter_of_block,
    block_destination,
    adapter_table_row,
):
    blocks = tokens.shape[0]
    steps = jnp.arange(blocks, dtype=jnp.int32)
    wide = jnp.arange(T, dtype=jnp.int32)
    dest_rep = block_destination // blocks
    slot = block_destination % blocks
    row = jnp.sum(
        jnp.where(adapter_of_block[:, None] == steps[None, :], adapter_table_row[None, :], 0), axis=1
    )
    adapter = row - dest_rep * 2
    before = (dest_rep[:, None] == dest_rep[None, :]) & (steps[None, :] < steps[:, None])
    place = dest_rep * 2 + jnp.sum(before.astype(jnp.int32), axis=1)
    hit = place[None, :] == steps[:, None]
    slot_at = jnp.sum(jnp.where(hit, slot[None, :], 0), axis=1)
    adapter_at = jnp.sum(jnp.where(hit, adapter[None, :], 0), axis=1)

    def by_token(v):
        return jnp.broadcast_to(v[:, None], (blocks, 8)).reshape(T)

    code = by_token(place) * 8 + wide % 8
    slot_code = by_token(slot_at) * 8 + wide % 8
    sel = (wide[:, None] == code[None, :]).astype(bf16)
    selt = (code[:, None] == wide[None, :]).astype(bf16)
    lab = jnp.concatenate(
        [
            (slot_code[:, None] == wide[None, :]).astype(bf16),
            (by_token(adapter_at)[:, None] == (wide // A)[None, :]).astype(bf16),
        ],
        axis=1,
    )
    q = jnp.asarray(rank_order(), bf16)

    vm = pl.BlockSpec(memory_space=pltpu.VMEM)
    hbm = pl.BlockSpec(memory_space=pl.ANY)
    dma = pltpu.SemaphoreType.DMA
    tg, val, dg, ug = pl.pallas_call(
        kernel,
        out_shape=(
            jax.ShapeDtypeStruct((T, D), bf16),
            jax.ShapeDtypeStruct((T, V), bf16),
            jax.ShapeDtypeStruct((A, DS), f32),
            jax.ShapeDtypeStruct((8, V), f32),
        ),
        in_specs=[hbm, vm, hbm, hbm, hbm, vm, vm, vm, vm],
        out_specs=(hbm, vm, vm, vm),
        scratch_shapes=[
            pltpu.VMEM((T, D), bf16),
            pltpu.VMEM((T, D), bf16),
            pltpu.VMEM((T, D), bf16),
            pltpu.VMEM((T, D), bf16),
            pltpu.VMEM((D, V), bf16),
            pltpu.VMEM((NF, 2, A, DS), bf16),
            pltpu.VMEM((A, V), f32),
            pltpu.VMEM((T, 2 * T), bf16),
            pltpu.VMEM((NF, A, DS), f32),
            pltpu.VMEM((4, 4, 64, DS), f32),
            pltpu.VMEM((4, 4, 64, DS), f32),
            pltpu.VMEM((4, 64, DS), f32),
            pltpu.VMEM((4, 64, DS), f32),
            pltpu.VMEM((4, 64, DS), f32),
            pltpu.VMEM((4, 64, DS), f32),
            pltpu.VMEM((A, V), f32),
            pltpu.VMEM((NF, 8, V), f32),
            pltpu.VMEM((T, V), bf16),
            pltpu.VMEM((T, V), bf16),
            pltpu.VMEM((T, 4 * A), bf16),
            pltpu.VMEM((T, 4 * A), bf16),
            pltpu.VMEM((2 * A, T), bf16),
            pltpu.VMEM((2 * A, V), bf16),
            pltpu.VMEM((T, V), f32),
            pltpu.VMEM((T, 2 * A), f32),
            dma((G,)),
            dma((G,)),
            dma((G,)),
            dma((2,)),
            dma((2,)),
            dma,
            dma((2,)),
            dma,
            dma((NF, 2)),
            dma,
            dma,
            dma((NF, 2)),
            dma,
            dma((NF,)),
            dma((4,)),
            dma((NF,)),
            dma((NF,)),
            dma((4,)),
            dma((4,)),
            dma((2,)),
            dma,
        ],
        compiler_params=pltpu.CompilerParams(
            collective_id=0, has_side_effects=True, vmem_limit_bytes=60 * 1024 * 1024
        ),
        cost_estimate=pl.CostEstimate(
            flops=14 * 10**9, bytes_accessed=12 * 2**20, transcendentals=0
        ),
        name="lora_moves",
    )(
        tokens.reshape(T, D),
        cotangent.reshape(T, V),
        frozen_weight,
        down_factor_table,
        up_factor_table.astype(f32).reshape(8, V),
        sel,
        selt,
        lab,
        q,
    )
    return (
        val.reshape(blocks, 8, V),
        tg.reshape(blocks, 8, D),
        dg.reshape(2, 64, DS),
        ug.reshape(2, 4, V),
    )


def solution(mesh):
    placed = (
        P("rep", "fsdp", None),
        P("rep", "fsdp", None),
        P("fsdp", None),
        P("rep", None, "fsdp"),
        P("rep", "fsdp", None),
        P("rep"),
        P("rep"),
        P(),
    )
    return jax.shard_map(
        local,
        mesh=mesh,
        in_specs=placed,
        out_specs=(
            P("rep", "fsdp", None),
            P("rep", "fsdp", None),
            P("rep", None, "fsdp"),
            P("rep", "fsdp", None),
        ),
        check_vma=False,
    )
```

time: 282 us -> 195 us (0.69)
  Pallas kernels: 267 us -> 180 us
    pallas_call x1, Pallas kernels: 267 us -> 180 us  [local(): pl.pallas_call(kernel, out_shape=(jax.ShapeDtypeStruct((T, D), bf16), jax...]
where the time goes in v2:
time: 195 us
  Pallas kernels  180 us (92%)
  local copies, waits for them, and re-layouts  10.5 us (5%)
  other arithmetic  3.46 us (2%)
    pallas_call x1, Pallas kernels, local(): pl.pallas_call(kernel, out_shape=(jax.ShapeDtypeStruct((T, D), bf16), jax...  180 us
    unnamed x5, local copies, waits for them, and re-layouts  7.25 us

profile of v2, /device:TPU:1, one launch (start us, length us, event | category | flops | bytes accessed | tf_op | source)
XLA Modules:
  0.0 194.9 jit_solution(8029815284968641554)
XLA Ops:
  0.6 0.9 select_reduce_fusion.1
  1.5 0.7 multiply_subtract_fusion
  2.2 0.2 convert_reduce_fusion
  2.3 0.1 select_reduce_fusion.2
  2.5 0.1 broadcast_in_dim.33
  2.5 0.1 mul.34
  2.7 0.1 broadcast_in_dim.30
  2.7 0.1 mul.32
  2.8 0.1 broadcast_in_dim.36
  2.9 0.1 eq.110
  3.0 1.3 reshape.108.up
  4.3 0.1 iota_compare_fusion
  4.5 0.7 add_convert_fusion.lab
  5.2 0.8 fusion.1
  6.0 180.3 %lora_moves.1 = (bf16[256,8192]{1,0:T(8,128)(2,1)}, bf16[256,1024]{1,0:T(8,128)(2,1)}, f32[128,512]{1,0:T(8,128)}, f32[8,1024]{1,0:T(8,128)}) custom-call(bf16[256,8192]{1,0:T(8,128)(2,1)} %bitcast.8, bf16[256,1024]{1,0:T(8,128)(2,1)} %bitcast.9, bf16[512,1024]{1,0:T(8,128)(2,1)} %w.1, bf16[2,64,512]{2,1,0:T(8,128)(2,1)} %down.1, f32[8,1024]{1,0:T(8,128)} %reshape.108.up, ...), custom_call_target="tpu_custom_call" | custom-call | flops 14000000000 | bytes 12582912 | tf_op jit(solution)/shard_map/lora_moves/pallas_call | solution.py:429
  186.3 1.4 reshape.106
  187.7 1.9 copy.16
  189.5 0.0 copy-start
  189.5 4.7 %copy.17 = bf16[32,8,8192]{2,1,0:T(8,128)(2,1)} copy(bf16[32,8,8192]{2,1,0:T(8,128)(2,1)} %bitcast.5) | data formatting | bytes 8388608
  194.2 0.0 copy-done
  194.2 0.7 copy.18
  (5 shorter events, 0.0 us)
Async XLA Ops:
  189.5 4.7 %copy-start = (f32[128,512]{1,0:T(8,128)S(1)}, f32[128,512]{1,0:T(8,128)}, u32[]{:S(2)}) copy-start(f32[128,512]{1,0:T(8,128)} %get-tuple-element.10) | copy-start | bytes 786436

commit v3 on v2

v3 whole, which is shorter than its diff:
```python
import functools

import jax
import jax.numpy as jnp
import numpy as np
from jax import lax
from jax.experimental import pallas as pl
from jax.experimental.pallas import tpu as pltpu
from jax.sharding import PartitionSpec as P

MESH = pl.DeviceIdType.MESH
bf16, f32 = jnp.bfloat16, jnp.float32

NR = 16
NF = 16
T = 256
RT = T // NR
D = 8192
V = 1024
DS = D // NF
HALF = DS // 2
QUARTER = HALF // 2
A = 128
G = 4
GC = D // G

REPS = [(dz, dc) for dz in (4, 3, 5, 2, 6, 1, 7) for dc in (0, 1)] + [(0, 1)]
RING = (1, 3, 2)
STEPS = (
    (),
    (
        ((1, 0), ((1, 0), (0, 1), (0, -1))),
        ((3, 0), ((0, 1), (0, -1))),
        ((0, 1), ((0, 1),)),
    ),
    (
        ((2, 0), ((0, 1), (0, -1))),
        ((1, 3), ((0, -1),)),
        ((3, 3), ((0, -1),)),
    ),
    (((2, 1), ((0, 1),)),),
)
PASSED = frozenset(off for step in STEPS for off, _ in step)
FAR = T // 2


def nt(a, b):
    return lax.dot_general(a, b, (((1,), (1,)), ((), ())), preferred_element_type=f32)


def tn(a, b):
    return lax.dot_general(a, b, (((0,), (0,)), ((), ())), preferred_element_type=f32)


def nn(a, b):
    return jnp.dot(a, b, preferred_element_type=f32)


def split(v):
    hi = v.astype(bf16)
    return hi, (v - hi.astype(f32)).astype(bf16)


ORDER = {0: 0, 1: 1, 7: 2, 6: 3, 3: 4, 4: 5, 2: 6, 5: 7}
NEAR = (0, 1, -1, -2)
OTHER = (0, 1, -1, 2)


def arrival_group(dz, dc, c):
    to = (c + dc) % 2
    up, low = ORDER[-dz % 8], ORDER[dz % 8]
    return 2 * (up + to * (low - up)) + dc


def kernel(
    tok, cot, w, down, up, sel, selt, lab, q,
    tg, val, dg, ug,
    xs, xr, gs, gr, wf, dn, ups, upc, upr, labr, dpart, ra, rb, sa, sb, ra2, rb2, upart, urecv,
    cotp, hc, hg, gtcat, upb, acc, mid,
    tok_sem, x_send, x_recv, lab_sem, hop_sem, hop_own, up_sem, dn_send, dn_recv, w_own, w_send, w_recv,
    sib_send, sib_recv, far_sem, g_send, g_recv, r_sem, r2_sem, u_sem, out_sem,
):
    rep, fs = lax.axis_index("rep"), lax.axis_index("fsdp")
    z, c, x, y = rep // 2, rep % 2, fs // 4, fs % 4
    plane = [((x + dx) % 4) * 4 + (y + dy) % 4 for dx in range(4) for dy in range(4)][1:]
    reps = [((z + dz) % 8) * 2 + (c + dc) % 2 for dz, dc in REPS]
    sib = rep + 1 - 2 * c
    turn = 3 - 6 * c
    opposite = ((z + turn + 8) % 8) * 2 + c
    partner = ((z - turn + 8) % 8) * 2 + c

    barrier = pltpu.get_barrier_semaphore()
    for r in reps:
        pl.semaphore_signal(barrier, inc=1, device_id=(r, fs), device_id_type=MESH)
    for f in plane:
        pl.semaphore_signal(barrier, inc=1, device_id=(rep, f), device_id_type=MESH)

    def group(g):
        return pl.ds(pl.multiple_of(g * GC, GC), GC)

    def loads(g):
        return pltpu.make_async_copy(tok.at[:, group(g)], gs.at[:, group(g)], tok_sem.at[g])

    for g in range(G):
        loads(g).start()
    own_w = pltpu.make_async_copy(w, wf.at[pl.ds(pl.multiple_of(fs * DS, DS), DS)], w_own)
    own_w.start()
    own_down = pltpu.make_async_copy(down, dn.at[fs, :, pl.ds(0, 64), :], hop_own)
    own_down.start()
    for a in range(2):
        ups[4 * a : 4 * a + 4, :] = up[a].astype(f32)

    for g in range(G):
        loads(g).wait()
        xs[:, group(g)] = nn(sel[...], gs[:, group(g)]).astype(bf16)
    pl.semaphore_wait(barrier, len(reps) + len(plane))

    def rows(r):
        return pl.ds(pl.multiple_of(r * RT, RT), RT)

    def push(src, dst, send, recv, r, f):
        pltpu.make_async_remote_copy(
            src_ref=src, dst_ref=dst, send_sem=send, recv_sem=recv,
            device_id=(r, f), device_id_type=MESH,
        ).start()

    def done(ref, sem):
        pltpu.make_async_copy(ref, ref, sem).wait()

    for (dz, dc), r in zip(REPS, reps):
        push(lab.at[rows(r)], labr.at[rows(arrival_group(dz, dc, c))], lab_sem.at[0], lab_sem.at[1], r, fs)
    pltpu.make_async_copy(lab.at[rows(rep)], labr.at[pl.ds(0, RT)], lab_sem.at[1]).start()
    push(ups.at[pl.ds(0, 8)], ups.at[pl.ds(8, 8)], up_sem.at[2], up_sem.at[3], opposite, fs)
    push(down, dn.at[fs, :, pl.ds(64, 64), :], hop_sem.at[0], hop_sem.at[1], opposite, fs)

    def wpart(f, h, core):
        return wf.at[pl.ds(pl.multiple_of(f * DS + core * HALF + h * QUARTER, QUARTER), QUARTER)]

    def push_w(f, h, to):
        push(wpart(f, h, c), wpart(f, h, c), w_send, w_recv.at[f, h], rep, to)

    def push_dn(f, h, to):
        push(dn.at[f, h], dn.at[f, h], dn_send, dn_recv.at[f, h], rep, to)

    def at(dx, dy):
        return ((x + dx + 4) % 4) * 4 + (y + dy + 4) % 4

    def source(off):
        return at(-off[0], -off[1])

    def ring(own_or, send):
        if own_or == 0:
            for d in (1, -1):
                send(source((0, 0)), 0, at(d, 0))
                send(source((0, 0)), 1, at(0, d))
            for d in (1, -1):
                send(source((0, 0)), 0, at(0, d))
                send(source((0, 0)), 1, at(d, 0))
        for off, goes in STEPS[own_or]:
            for h in (0, 1):
                o = off if h == 0 else off[::-1]
                ref, sem = unit(send, source(o), h)
                done(ref, sem)
                for to in goes:
                    t = to if h == 0 else to[::-1]
                    send(source(o), h, at(*t))

    def unit(send, f, h):
        if send is push_w:
            return wpart(f, h, c), w_recv.at[f, h]
        return dn.at[f, h], dn_recv.at[f, h]

    own_w.wait()
    ring(0, push_w)

    def tokens_off(g):
        for (dz, dc), r in zip(REPS, reps):
            push(
                xs.at[rows(r), group(g)], xr.at[rows(arrival_group(dz, dc, c)), group(g)],
                x_send.at[g], x_recv.at[g], r, fs,
            )
        pltpu.make_async_copy(
            xs.at[rows(rep), group(g)], xr.at[pl.ds(0, RT), group(g)], x_recv.at[g]
        ).start()

    tokens_off(0)

    done(labr, lab_sem.at[1])
    cotp[:, :V] = nn(labr[:, :T], cot[...]).astype(bf16)
    cotp[:, V:] = labr[:, T:]
    far = pl.ds(FAR, FAR)
    push(cotp.at[far], hc.at[far], far_sem.at[0], far_sem.at[1], opposite, fs)
    hc[:FAR, :] = cotp[:FAR, :]
    tokens_off(1)

    done(ups.at[pl.ds(0, 8)], up_sem.at[3])
    upc[...] = ups[...].astype(bf16)
    mine16 = pl.ds(pl.multiple_of(fs * 16, 16), 16)
    for f in plane:
        push(upc, upr.at[mine16], up_sem.at[0], up_sem.at[1], rep, f)
    upr[mine16, :] = upc[...]
    own_down.wait()
    done(dn.at[0, :, pl.ds(0, 64), :], hop_sem.at[1])
    ring(0, push_dn)
    tokens_off(2)
    tokens_off(3)

    done(upr.at[pl.ds(0, 15 * 16)], up_sem.at[1])
    upb[...] = nn(q[...], upr[...]).astype(bf16)
    lane = lax.broadcasted_iota(jnp.int32, (T, 2 * A), 1)
    row = lax.broadcasted_iota(jnp.int32, (T, 2 * A), 0)
    second = (lane % A) >= 64

    def chosen(ref):
        ids = ref[:, V:].astype(f32)
        return jnp.concatenate([1.0 - ids, ids], axis=1)

    mask = jnp.where(second, 0.0, chosen(cotp))
    backt = (2.0 * nt(cotp[:, :V], upb[...]) * mask).T
    hi, lo = split(jnp.concatenate([backt[0:64], backt[128:192]], axis=0))
    gtcat[:A, :] = hi
    gtcat[A:, :] = lo
    done(hc.at[far], far_sem.at[1])
    back = jnp.where(second == (row >= FAR), 2.0 * nt(hc[:, :V], upb[...]) * chosen(hc), 0.0)
    hi, lo = split(back)
    hg[:, : 2 * A] = hi
    hg[:, 2 * A :] = lo

    def dcols(f):
        return pl.ds(pl.multiple_of(f * DS, DS), DS)

    owner, other = rep, partner
    back_to = []
    for k in range(4):
        for dc in (0, 1):
            core = (c + dc) % 2
            way = 1 - 2 * c
            back_to.append((2 * k + dc, ((z + way * NEAR[k] + 8) % 8) * 2 + core, owner))
            back_to.append((8 + 2 * k + dc, ((z + way * OTHER[k] + 8) % 8) * 2 + core, other))
    remote = [e for e in back_to if e[0] not in (0, 8)]
    remote = remote[::-1]

    def grads(f):
        dv = dn[f].reshape(2 * A, DS)
        out = nt(hc[:, :V], wf[dcols(f), :])
        out = out + nn(hg[:, : 2 * A], dv) + nn(hg[:, 2 * A :], dv)
        gs[:, dcols(f)] = out.astype(bf16)

    def grads_off(g):
        for k, r, place in remote:
            push(
                gs.at[pl.ds(k * RT, RT), group(g)], gr.at[rows(place), group(g)],
                g_send.at[g], g_recv.at[g], r, fs,
            )
        for k, place in ((0, owner), (8, other)):
            pltpu.make_async_copy(
                gs.at[pl.ds(k * RT, RT), group(g)], gr.at[rows(place), group(g)], g_recv.at[g]
            ).start()

    def whalf(f, core):
        return wf.at[pl.ds(pl.multiple_of(f * DS + core * HALF, HALF), HALF)]

    def take_in(offs):
        for off in offs:
            f = source(off)
            for h in (0, 1):
                if (off if h == 0 else off[::-1]) not in PASSED:
                    done(wpart(f, h, c), w_recv.at[f, h])
                    done(dn.at[f, h], dn_recv.at[f, h])
            push(whalf(f, c), whalf(f, c), sib_send, sib_recv.at[f], sib, fs)

    def grads_of(count, dx, dy):
        def step(i, _):
            f = ((x + 4 - dx(i)) % 4) * 4 + (y + 4 - dy(i)) % 4
            done(whalf(f, 1 - c), sib_recv.at[f])
            grads(f)
            return 0

        lax.fori_loop(0, count, step, 0)

    def down_terms(g):
        def term(k, _):
            fy = (y + k) % 4
            f = g * 4 + fy
            part = nn(gtcat[...], xr[:, dcols(f)])
            dpart[f] = part[:A] + part[A:]

            @pl.when(g != x)
            def _():
                push(dpart.at[f, pl.ds(0, 64)], ra.at[x, fy], r_sem.at[0], r_sem.at[1], rep, g * 4 + y)

            @pl.when(fy != y)
            def _():
                push(dpart.at[f, pl.ds(64, 64)], rb.at[y, g], r_sem.at[2], r_sem.at[3], rep, x * 4 + fy)

            return 0

        lax.fori_loop(0, 4, term, 0)

    def odd(i):
        return 1 + 2 * (i % 2)

    ring(1, push_w)
    ring(1, push_dn)
    take_in([(1, 0), (3, 0), (0, 1), (0, 3)])
    grads(fs)
    grads_of(4, lambda i: odd(i) * (1 - i // 2), lambda i: odd(i) * (i // 2))
    ring(2, push_w)
    ring(2, push_dn)
    take_in([(2, 0), (0, 2), (1, 1), (3, 1), (1, 3), (3, 3)])
    grads_of(2, lambda i: 2 - 2 * i, lambda i: 2 * i)
    ring(3, push_w)
    ring(3, push_dn)
    grads_of(4, lambda i: odd(i), lambda i: 1 + 2 * (i // 2))
    take_in([(2, 1), (2, 3), (1, 2), (3, 2), (2, 2)])
    grads_of(4, lambda i: 2 - (1 - 2 * (i % 2)) * (i // 2), lambda i: odd(i) + (2 - odd(i)) * (i // 2))
    grads_of(1, lambda i: 2, lambda i: 2)

    def arrived(g, _):
        done(xr.at[:, group(g)], x_recv.at[g])
        grads_off(g)
        down_terms(g)
        return 0

    lax.fori_loop(0, G, arrived, 0)

    acc[...] = jnp.zeros_like(acc)
    mid[...] = jnp.zeros_like(mid)

    def fwd(g, _):
        acc[...] += nn(xr[:, group(g)], wf[group(g), :])
        return 0

    def low(f, _):
        mid[...] += nt(xr[:, dcols(f)], dn[f].reshape(2 * A, DS))
        return 0

    lax.fori_loop(0, G, fwd, 0)
    lax.fori_loop(0, NF, low, 0)

    m2 = 2.0 * mid[...] * mask
    hi, lo = split(m2)
    out = acc[...] + nn(hi, upb[...]) + nn(lo, upb[...])
    val[...] = tn(labr[:, :T], out.astype(bf16)).astype(bf16)
    hi, lo = split(m2.T)
    hi = tn(q[...], hi).astype(bf16)
    lo = tn(q[...], lo).astype(bf16)
    own_cot = cotp[:, :V]
    upart[...] = nn(hi, own_cot) + nn(lo, own_cot)
    for f in plane:
        push(upart.at[pl.ds(pl.multiple_of(f * 16, 16), 8)], urecv.at[fs], u_sem.at[0], u_sem.at[1], rep, f)
    mine8 = pl.ds(pl.multiple_of(fs * 16, 16), 8)
    pltpu.make_async_copy(upart.at[mine8], urecv.at[fs], u_sem.at[1]).start()

    done(ra.at[pl.ds(0, 3)], r_sem.at[1])
    done(rb.at[pl.ds(0, 3)], r_sem.at[3])

    def first_sum(k, _):
        own_a, own_b = dpart[x * 4 + k, :64, :], dpart[k * 4 + y, 64:, :]
        for d in RING:
            own_a = own_a + ra[(x + d) % 4, k]
            own_b = own_b + rb[(y + d) % 4, k]
        sa[k] = own_a
        sb[k] = own_b

        @pl.when(k != y)
        def _():
            push(sa.at[k], ra2.at[y], r2_sem.at[0], r2_sem.at[1], rep, x * 4 + k)

        @pl.when(k != x)
        def _():
            push(sb.at[k], rb2.at[x], r2_sem.at[2], r2_sem.at[3], rep, k * 4 + y)

        return 0

    lax.fori_loop(0, 4, first_sum, 0)

    for g in range(G):
        done(xs.at[pl.ds(0, T - RT), group(g)], x_send.at[g])

    def finish(g, _):
        done(gr.at[:, group(g)], g_recv.at[g])
        xs[:, group(g)] = nn(selt[...], gr[:, group(g)]).astype(bf16)
        pltpu.make_async_copy(xs.at[:, group(g)], tg.at[:, group(g)], out_sem).start()
        return 0

    lax.fori_loop(0, G, finish, 0)

    done(urecv, u_sem.at[1])
    up_total = jnp.sum(urecv[...], axis=0)
    for a in range(2):
        ug[a] = up_total[4 * a : 4 * a + 4]
    done(ra2.at[pl.ds(0, 3)], r2_sem.at[1])
    done(rb2.at[pl.ds(0, 3)], r2_sem.at[3])
    sum_a, sum_b = sa[y], sb[x]
    for d in RING:
        sum_a = sum_a + ra2[(y + d) % 4]
        sum_b = sum_b + rb2[(x + d) % 4]
    dg[0] = sum_a
    dg[1] = sum_b

    done(tg, out_sem)
    done(lab.at[pl.ds(0, T - RT)], lab_sem.at[0])
    done(down, hop_sem.at[0])
    done(cotp.at[far], far_sem.at[0])
    done(upr.at[pl.ds(0, 15 * 16)], up_sem.at[0])
    done(ups.at[pl.ds(0, 8)], up_sem.at[2])
    done(dn.at[pl.ds(0, 15)], dn_send)
    done(wf.at[pl.ds(0, 30 * QUARTER)], w_send)
    done(wf.at[pl.ds(0, 15 * HALF)], sib_send)
    done(ra.at[pl.ds(0, 3)], r_sem.at[0])
    done(rb.at[pl.ds(0, 3)], r_sem.at[2])
    done(ra2.at[pl.ds(0, 3)], r2_sem.at[0])
    done(rb2.at[pl.ds(0, 3)], r2_sem.at[2])
    done(upart.at[pl.ds(0, 15 * 8)], u_sem.at[0])

    for g in range(G):
        done(gs.at[pl.ds(0, 14 * RT), group(g)], g_send.at[g])


def rank_order():
    order = np.zeros((2 * A, 2 * A), np.float32)
    for k in range(2 * A):
        a, d, r = k // A, k // 64 % 2, k % 64
        order[k, (r // 4) * 16 + d * 8 + a * 4 + r % 4] = 1.0
    return order


def local(
    tokens,
    cotangent,
    frozen_weight,
    down_factor_table,
    up_factor_table,
    adapter_of_block,
    block_destination,
    adapter_table_row,
):
    blocks = tokens.shape[0]
    steps = jnp.arange(blocks, dtype=jnp.int32)
    wide = jnp.arange(T, dtype=jnp.int32)
    dest_rep = block_destination // blocks
    slot = block_destination % blocks
    row = jnp.sum(
        jnp.where(adapter_of_block[:, None] == steps[None, :], adapter_table_row[None, :], 0), axis=1
    )
    adapter = row - dest_rep * 2
    before = (dest_rep[:, None] == dest_rep[None, :]) & (steps[None, :] < steps[:, None])
    place = dest_rep * 2 + jnp.sum(before.astype(jnp.int32), axis=1)
    hit = place[None, :] == steps[:, None]
    slot_at = jnp.sum(jnp.where(hit, slot[None, :], 0), axis=1)
    adapter_at = jnp.sum(jnp.where(hit, adapter[None, :], 0), axis=1)

    def by_token(v):
        return jnp.broadcast_to(v[:, None], (blocks, 8)).reshape(T)

    code = by_token(place) * 8 + wide % 8
    slot_code = by_token(slot_at) * 8 + wide % 8
    sel = (wide[:, None] == code[None, :]).astype(bf16)
    selt = (code[:, None] == wide[None, :]).astype(bf16)
    lab = jnp.concatenate(
        [
            (slot_code[:, None] == wide[None, :]).astype(bf16),
            jnp.broadcast_to(by_token(adapter_at)[:, None], (T, A)).astype(bf16),
        ],
        axis=1,
    )
    q = jnp.asarray(rank_order(), bf16)

    vm = pl.BlockSpec(memory_space=pltpu.VMEM)
    hbm = pl.BlockSpec(memory_space=pl.ANY)
    dma = pltpu.SemaphoreType.DMA
    tg, val, dg, ug = pl.pallas_call(
        kernel,
        out_shape=(
            jax.ShapeDtypeStruct((T, D), bf16),
            jax.ShapeDtypeStruct((T, V), bf16),
            jax.ShapeDtypeStruct((2, 64, DS), f32),
            jax.ShapeDtypeStruct((2, 4, V), f32),
        ),
        in_specs=[hbm, vm, hbm, hbm, vm, vm, vm, vm, vm],
        out_specs=(hbm, vm, vm, vm),
        scratch_shapes=[
            pltpu.VMEM((T, D), bf16),
            pltpu.VMEM((T, D), bf16),
            pltpu.VMEM((T, D), bf16),
            pltpu.VMEM((T, D), bf16),
            pltpu.VMEM((D, V), bf16),
            pltpu.VMEM((NF, 2, A, DS), bf16),
            pltpu.VMEM((16, V), f32),
            pltpu.VMEM((16, V), bf16),
            pltpu.VMEM((2 * A, V), bf16),
            pltpu.VMEM((T, T + A), bf16),
            pltpu.VMEM((NF, A, DS), f32),
            pltpu.VMEM((4, 4, 64, DS), f32),
            pltpu.VMEM((4, 4, 64, DS), f32),
            pltpu.VMEM((4, 64, DS), f32),
            pltpu.VMEM((4, 64, DS), f32),
            pltpu.VMEM((4, 64, DS), f32),
            pltpu.VMEM((4, 64, DS), f32),
            pltpu.VMEM((2 * A, V), f32),
            pltpu.VMEM((NF, 8, V), f32),
            pltpu.VMEM((T, V + A), bf16),
            pltpu.VMEM((T, V + A), bf16),
            pltpu.VMEM((T, 4 * A), bf16),
            pltpu.VMEM((2 * A, T), bf16),
            pltpu.VMEM((2 * A, V), bf16),
            pltpu.VMEM((T, V), f32),
            pltpu.VMEM((T, 2 * A), f32),
            dma((G,)),
            dma((G,)),
            dma((G,)),
            dma((2,)),
            dma((2,)),
            dma,
            dma((4,)),
            dma,
            dma((NF, 2)),
            dma,
            dma,
            dma((NF, 2)),
            dma,
            dma((NF,)),
            dma((2,)),
            dma((G,)),
            dma((G,)),
            dma((4,)),
            dma((4,)),
            dma((2,)),
            dma,
        ],
        compiler_params=pltpu.CompilerParams(
            collective_id=0, has_side_effects=True, vmem_limit_bytes=60 * 1024 * 1024
        ),
        cost_estimate=pl.CostEstimate(
            flops=14 * 10**9, bytes_accessed=12 * 2**20, transcendentals=0
        ),
        name="lora_moves",
    )(
        tokens.reshape(T, D),
        cotangent.reshape(T, V),
        frozen_weight,
        down_factor_table,
        up_factor_table,
        sel,
        selt,
        lab,
        q,
    )
    return (
        val.reshape(blocks, 8, V),
        tg.reshape(blocks, 8, D),
        dg,
        ug,
    )


def solution(mesh):
    placed = (
        P("rep", "fsdp", None),
        P("rep", "fsdp", None),
        P("fsdp", None),
        P("rep", None, "fsdp"),
        P("rep", "fsdp", None),
        P("rep"),
        P("rep"),
        P(),
    )
    return jax.shard_map(
        local,
        mesh=mesh,
        in_specs=placed,
        out_specs=(
            P("rep", "fsdp", None),
            P("rep", "fsdp", None),
            P("rep", None, "fsdp"),
            P("rep", "fsdp", None),
        ),
        check_vma=False,
    )
```

time: 195 us -> 187 us (0.959)
  Pallas kernels: 180 us -> 174 us
  local copies, waits for them, and re-layouts: 10.5 us -> 8.46 us
    pallas_call x1, Pallas kernels: 180 us -> 174 us  [local(): pl.pallas_call(kernel, out_shape=(jax.ShapeDtypeStruct((T, D), bf16), jax...]
    reshape x2 -> x0, local copies, waits for them, and re-layouts: 2.73 us -> none  [the longest x1 1.39 us: local(): ug.reshape(2, 4, V)]
    unnamed x5 -> x8, local copies, waits for them, and re-layouts: 7.25 us -> 7.87 us
where the time goes in v3:
time: 187 us
  Pallas kernels  174 us (93%)
  local copies, waits for them, and re-layouts  8.46 us (5%)
  other arithmetic  3.4 us (2%)
    pallas_call x1, Pallas kernels, local(): pl.pallas_call(kernel, out_shape=(jax.ShapeDtypeStruct((T, D), bf16), jax...  174 us
    unnamed x8, local copies, waits for them, and re-layouts  7.87 us

profile of v3, /device:TPU:1, one launch (start us, length us, event | category | flops | bytes accessed | tf_op | source)
XLA Modules:
  0.0 186.6 jit_solution(6871065723817005997)
XLA Ops:
  0.6 0.9 select_reduce_fusion.1
  1.5 0.7 multiply_subtract_fusion
  2.2 0.2 convert_reduce_fusion
  2.3 0.1 select_reduce_fusion.2
  2.5 0.1 broadcast_in_dim.38
  2.6 0.1 convert_element_type.25
  2.7 0.1 broadcast_in_dim.35
  2.7 0.1 mul.34
  2.8 0.1 broadcast_in_dim.32
  2.9 0.1 mul.32
  3.0 0.1 broadcast_in_dim.39
  3.1 0.1 fusion.2
  3.2 0.7 pad_maximum_fusion.lab
  3.9 0.8 fusion.1
  4.7 174.0 %lora_moves.1 = (bf16[256,8192]{1,0:T(8,128)(2,1)}, bf16[256,1024]{1,0:T(8,128)(2,1)}, f32[2,64,512]{2,1,0:T(8,128)}, f32[2,4,1024]{2,1,0:T(4,128)}) custom-call(bf16[256,8192]{1,0:T(8,128)(2,1)} %bitcast.6, bf16[256,1024]{1,0:T(8,128)(2,1)} %bitcast.7, bf16[512,1024]{1,0:T(8,128)(2,1)} %w.1, bf16[2,64,512]{2,1,0:T(8,128)(2,1)} %down.1, ...), custom_call_target="tpu_custom_call" | custom-call | flops 14000000000 | bytes 12582912 | tf_op jit(solution)/shard_map/lora_moves/pallas_call | solution.py:473
  178.7 1.9 %copy.17 = bf16[32,8,1024]{2,1,0:T(8,128)(2,1)} copy(bf16[32,8,1024]{2,1,0:T(8,128)(2,1)} %bitcast.5) | data formatting | bytes 1048576
  180.5 0.0 copy-start
  180.5 0.0 copy-start.1
  180.6 4.7 %copy.18 = bf16[32,8,8192]{2,1,0:T(8,128)(2,1)} copy(bf16[32,8,8192]{2,1,0:T(8,128)(2,1)} %bitcast.4) | data formatting | bytes 8388608
  185.2 0.0 copy-done
  185.2 0.7 copy.19
  185.9 0.0 copy-done.1
  185.9 0.6 copy.20
  (5 shorter events, 0.0 us)
Async XLA Ops:
  180.5 4.7 %copy-start = (f32[2,64,512]{2,1,0:T(8,128)S(1)}, f32[2,64,512]{2,1,0:T(8,128)}, u32[]{:S(2)}) copy-start(f32[2,64,512]{2,1,0:T(8,128)} %get-tuple-element.27) | copy-start | bytes 786436
  180.5 5.4 %copy-start.1 = (f32[2,4,1024]{2,1,0:T(4,128)S(1)}, f32[2,4,1024]{2,1,0:T(4,128)}, u32[]{:S(2)}) copy-start(f32[2,4,1024]{2,1,0:T(4,128)} %get-tuple-element.28) | copy-start | bytes 98308

commit v4 on v3

--- a/solution.py
+++ b/solution.py
@@ -41,7 +41,6 @@
     (((2, 1), ((0, 1),)),),
 )
 PASSED = frozenset(off for step in STEPS for off, _ in step)
-FAR = T // 2
 
 
 def nt(a, b):
@@ -61,19 +60,21 @@
     return hi, (v - hi.astype(f32)).astype(bf16)
 
 
-ORDER = {0: 0, 1: 1, 7: 2, 6: 3, 3: 4, 4: 5, 2: 6, 5: 7}
-NEAR = (0, 1, -1, -2)
-OTHER = (0, 1, -1, 2)
+ORDER = {0: 0, 1: 2, 7: 4, 3: 6, 2: 8, 5: 11, 6: 13}
+OPPOSITE = (10, 15)
+CUTS = (0, 96, 176, 256)
+K3 = 192
 
 
 def arrival_group(dz, dc, c):
-    to = (c + dc) % 2
-    up, low = ORDER[-dz % 8], ORDER[dz % 8]
-    return 2 * (up + to * (low - up)) + dc
+    above = -dz % 8
+    if above == 4:
+        return OPPOSITE[0] + c * (OPPOSITE[1] - OPPOSITE[0])
+    return ORDER[above] + dc
 
 
 def kernel(
-    tok, cot, w, down, up, sel, selt, lab, q,
+    tok, cot, w, down, up, sel, selt, lab, q, q8,
     tg, val, dg, ug,
     xs, xr, gs, gr, wf, dn, ups, upc, upr, labr, dpart, ra, rb, sa, sb, ra2, rb2, upart, urecv,
     cotp, hc, hg, gtcat, upb, acc, mid,
@@ -85,9 +86,7 @@
     plane = [((x + dx) % 4) * 4 + (y + dy) % 4 for dx in range(4) for dy in range(4)][1:]
     reps = [((z + dz) % 8) * 2 + (c + dc) % 2 for dz, dc in REPS]
     sib = rep + 1 - 2 * c
-    turn = 3 - 6 * c
-    opposite = ((z + turn + 8) % 8) * 2 + c
-    partner = ((z - turn + 8) % 8) * 2 + c
+    above, below = ((z + 3) % 8) * 2 + c, ((z + 5) % 8) * 2 + c
 
     barrier = pltpu.get_barrier_semaphore()
     for r in reps:
@@ -109,6 +108,7 @@
     own_down.start()
     for a in range(2):
         ups[4 * a : 4 * a + 4, :] = up[a].astype(f32)
+    ups[24:, :] = jnp.zeros((8, V), f32)
 
     for g in range(G):
         loads(g).wait()
@@ -130,8 +130,9 @@
     for (dz, dc), r in zip(REPS, reps):
         push(lab.at[rows(r)], labr.at[rows(arrival_group(dz, dc, c))], lab_sem.at[0], lab_sem.at[1], r, fs)
     pltpu.make_async_copy(lab.at[rows(rep)], labr.at[pl.ds(0, RT)], lab_sem.at[1]).start()
-    push(ups.at[pl.ds(0, 8)], ups.at[pl.ds(8, 8)], up_sem.at[2], up_sem.at[3], opposite, fs)
-    push(down, dn.at[fs, :, pl.ds(64, 64), :], hop_sem.at[0], hop_sem.at[1], opposite, fs)
+    for k, r in ((1, above), (2, below)):
+        push(ups.at[pl.ds(0, 8)], ups.at[pl.ds(8 * k, 8)], up_sem.at[2], up_sem.at[2 + k], r, fs)
+        push(down, dn.at[fs, :, pl.ds(64 * k, 64), :], hop_sem.at[0], hop_sem.at[k], r, fs)
 
     def wpart(f, h, core):
         return wf.at[pl.ds(pl.multiple_of(f * DS + core * HALF + h * QUARTER, QUARTER), QUARTER)]
@@ -188,62 +189,68 @@
     done(labr, lab_sem.at[1])
     cotp[:, :V] = nn(labr[:, :T], cot[...]).astype(bf16)
     cotp[:, V:] = labr[:, T:]
-    far = pl.ds(FAR, FAR)
-    push(cotp.at[far], hc.at[far], far_sem.at[0], far_sem.at[1], opposite, fs)
-    hc[:FAR, :] = cotp[:FAR, :]
+    served = [pl.ds(CUTS[k], CUTS[k + 1] - CUTS[k]) for k in range(3)]
+    for k, r in ((1, above), (2, below)):
+        push(cotp.at[served[k]], hc.at[served[k]], far_sem.at[0], far_sem.at[k], r, fs)
+    hc[served[0], :] = cotp[served[0], :]
     tokens_off(1)
 
     done(ups.at[pl.ds(0, 8)], up_sem.at[3])
+    done(ups.at[pl.ds(0, 8)], up_sem.at[4])
     upc[...] = ups[...].astype(bf16)
-    mine16 = pl.ds(pl.multiple_of(fs * 16, 16), 16)
+    mine32 = pl.ds(pl.multiple_of(fs * 32, 32), 32)
     for f in plane:
-        push(upc, upr.at[mine16], up_sem.at[0], up_sem.at[1], rep, f)
-    upr[mine16, :] = upc[...]
+        push(upc, upr.at[mine32], up_sem.at[0], up_sem.at[1], rep, f)
+    upr[mine32, :] = upc[...]
     own_down.wait()
-    done(dn.at[0, :, pl.ds(0, 64), :], hop_sem.at[1])
+    done(down, hop_sem.at[1])
+    done(down, hop_sem.at[2])
     ring(0, push_dn)
     tokens_off(2)
     tokens_off(3)
 
-    done(upr.at[pl.ds(0, 15 * 16)], up_sem.at[1])
+    done(upr.at[pl.ds(0, 15 * 32)], up_sem.at[1])
     upb[...] = nn(q[...], upr[...]).astype(bf16)
-    lane = lax.broadcasted_iota(jnp.int32, (T, 2 * A), 1)
-    row = lax.broadcasted_iota(jnp.int32, (T, 2 * A), 0)
-    second = (lane % A) >= 64
-
-    def chosen(ref):
-        ids = ref[:, V:].astype(f32)
-        return jnp.concatenate([1.0 - ids, ids], axis=1)
-
-    mask = jnp.where(second, 0.0, chosen(cotp))
-    backt = (2.0 * nt(cotp[:, :V], upb[...]) * mask).T
-    hi, lo = split(jnp.concatenate([backt[0:64], backt[128:192]], axis=0))
+    own_up = jnp.concatenate([upb[:64, :], upb[K3 : K3 + 64, :]], axis=0)
+    ids = cotp[:, V:].astype(f32)
+    mask = jnp.where(lax.broadcasted_iota(jnp.int32, (T, A), 1) < 64, 1.0 - ids, ids)
+    hi, lo = split((2.0 * nt(cotp[:, :V], own_up) * mask).T)
     gtcat[:A, :] = hi
     gtcat[A:, :] = lo
-    done(hc.at[far], far_sem.at[1])
-    back = jnp.where(second == (row >= FAR), 2.0 * nt(hc[:, :V], upb[...]) * chosen(hc), 0.0)
+    done(hc.at[served[1]], far_sem.at[1])
+    done(hc.at[served[2]], far_sem.at[2])
+    lane = lax.broadcasted_iota(jnp.int32, (T, 2 * K3), 1)
+    row = lax.broadcasted_iota(jnp.int32, (T, 2 * K3), 0)
+    owner_at = jnp.where(row >= CUTS[2], 2, jnp.where(row >= CUTS[1], 1, 0))
+    ids = hc[:, V:].astype(f32)
+    ids = jnp.concatenate([ids, ids, ids], axis=1)
+    chosen = jnp.where(lane < K3, 1.0 - ids, ids)
+    lane = jnp.where(lane < K3, lane, lane - K3)
+    at_lane = jnp.where(lane >= 128, 2, jnp.where(lane >= 64, 1, 0))
+    back = jnp.where(at_lane == owner_at, 2.0 * nt(hc[:, :V], upb[...]) * chosen, 0.0)
     hi, lo = split(back)
-    hg[:, : 2 * A] = hi
-    hg[:, 2 * A :] = lo
+    hg[:, : 2 * K3] = hi
+    hg[:, 2 * K3 :] = lo
 
     def dcols(f):
         return pl.ds(pl.multiple_of(f * DS, DS), DS)
 
-    owner, other = rep, partner
     back_to = []
-    for k in range(4):
-        for dc in (0, 1):
-            core = (c + dc) % 2
-            way = 1 - 2 * c
-            back_to.append((2 * k + dc, ((z + way * NEAR[k] + 8) % 8) * 2 + core, owner))
-            back_to.append((8 + 2 * k + dc, ((z + way * OTHER[k] + 8) % 8) * 2 + core, other))
-    remote = [e for e in back_to if e[0] not in (0, 8)]
+    for dc in (0, 1):
+        core = (c + dc) % 2
+        for k, dz, place in (
+            (0, 0, rep), (2, 1, rep), (4, 7, rep), (6, 0, below), (8, 7, below), (11, 0, above), (13, 1, above),
+        ):
+            back_to.append((k + dc, ((z + dz) % 8) * 2 + core, place))
+    back_to.append((OPPOSITE[0], ((z + 1) % 8) * 2, below))
+    back_to.append((OPPOSITE[1], ((z + 7) % 8) * 2 + 1, above))
+    remote = [e for e in back_to if e[0] not in (0, 6, 11)]
     remote = remote[::-1]
 
     def grads(f):
-        dv = dn[f].reshape(2 * A, DS)
+        dv = dn[f].reshape(2 * K3, DS)
         out = nt(hc[:, :V], wf[dcols(f), :])
-        out = out + nn(hg[:, : 2 * A], dv) + nn(hg[:, 2 * A :], dv)
+        out = out + nn(hg[:, : 2 * K3], dv) + nn(hg[:, 2 * K3 :], dv)
         gs[:, dcols(f)] = out.astype(bf16)
 
     def grads_off(g):
@@ -252,7 +259,7 @@
                 gs.at[pl.ds(k * RT, RT), group(g)], gr.at[rows(place), group(g)],
                 g_send.at[g], g_recv.at[g], r, fs,
             )
-        for k, place in ((0, owner), (8, other)):
+        for k, place in ((0, rep), (6, below), (11, above)):
             pltpu.make_async_copy(
                 gs.at[pl.ds(k * RT, RT), group(g)], gr.at[rows(place), group(g)], g_recv.at[g]
             ).start()
@@ -318,10 +325,15 @@
 
     def arrived(g, _):
         done(xr.at[:, group(g)], x_recv.at[g])
-        grads_off(g)
+
+        @pl.when(g + 1 < G)
+        def _():
+            grads_off(g + 1)
+
         down_terms(g)
         return 0
 
+    grads_off(0)
     lax.fori_loop(0, G, arrived, 0)
 
     acc[...] = jnp.zeros_like(acc)
@@ -332,7 +344,7 @@
         return 0
 
     def low(f, _):
-        mid[...] += nt(xr[:, dcols(f)], dn[f].reshape(2 * A, DS))
+        mid[...] += nt(xr[:, dcols(f)], dn[f, :, pl.ds(0, 64), :].reshape(A, DS))
         return 0
 
     lax.fori_loop(0, G, fwd, 0)
@@ -340,16 +352,16 @@
 
     m2 = 2.0 * mid[...] * mask
     hi, lo = split(m2)
-    out = acc[...] + nn(hi, upb[...]) + nn(lo, upb[...])
+    out = acc[...] + nn(hi, own_up) + nn(lo, own_up)
     val[...] = tn(labr[:, :T], out.astype(bf16)).astype(bf16)
     hi, lo = split(m2.T)
-    hi = tn(q[...], hi).astype(bf16)
-    lo = tn(q[...], lo).astype(bf16)
+    hi = tn(q8[...], hi).astype(bf16)
+    lo = tn(q8[...], lo).astype(bf16)
     own_cot = cotp[:, :V]
     upart[...] = nn(hi, own_cot) + nn(lo, own_cot)
     for f in plane:
-        push(upart.at[pl.ds(pl.multiple_of(f * 16, 16), 8)], urecv.at[fs], u_sem.at[0], u_sem.at[1], rep, f)
-    mine8 = pl.ds(pl.multiple_of(fs * 16, 16), 8)
+        push(upart.at[pl.ds(pl.multiple_of(f * 8, 8), 8)], urecv.at[fs], u_sem.at[0], u_sem.at[1], rep, f)
+    mine8 = pl.ds(pl.multiple_of(fs * 8, 8), 8)
     pltpu.make_async_copy(upart.at[mine8], urecv.at[fs], u_sem.at[1]).start()
 
     done(ra.at[pl.ds(0, 3)], r_sem.at[1])
@@ -401,10 +413,10 @@
 
     done(tg, out_sem)
     done(lab.at[pl.ds(0, T - RT)], lab_sem.at[0])
-    done(down, hop_sem.at[0])
-    done(cotp.at[far], far_sem.at[0])
-    done(upr.at[pl.ds(0, 15 * 16)], up_sem.at[0])
-    done(ups.at[pl.ds(0, 8)], up_sem.at[2])
+    done(dn.at[0, :, pl.ds(0, 128), :], hop_sem.at[0])
+    done(cotp.at[pl.ds(CUTS[1], T - CUTS[1])], far_sem.at[0])
+    done(upr.at[pl.ds(0, 15 * 32)], up_sem.at[0])
+    done(ups.at[pl.ds(0, 16)], up_sem.at[2])
     done(dn.at[pl.ds(0, 15)], dn_send)
     done(wf.at[pl.ds(0, 30 * QUARTER)], w_send)
     done(wf.at[pl.ds(0, 15 * HALF)], sib_send)
@@ -415,15 +427,24 @@
     done(upart.at[pl.ds(0, 15 * 8)], u_sem.at[0])
 
     for g in range(G):
-        done(gs.at[pl.ds(0, 14 * RT), group(g)], g_send.at[g])
-
-
-def rank_order():
-    order = np.zeros((2 * A, 2 * A), np.float32)
-    for k in range(2 * A):
-        a, d, r = k // A, k // 64 % 2, k % 64
-        order[k, (r // 4) * 16 + d * 8 + a * 4 + r % 4] = 1.0
-    return order
+        done(gs.at[pl.ds(0, 13 * RT), group(g)], g_send.at[g])
+
+
+def settle(tg, val, dg, ug, tg_out, val_out, dg_out, ug_out):
+    tg_out[...] = tg[...]
+    val_out[...] = val[...]
+    dg_out[...] = dg[...]
+    ug_out[...] = ug[...]
+
+
+def rank_orders():
+    three, one = np.zeros((2 * K3, 32 * NF), np.float32), np.zeros((A, A), np.float32)
+    for a in range(2):
+        for r in range(64):
+            for d in range(3):
+                three[a * K3 + d * 64 + r, (r // 4) * 32 + d * 8 + a * 4 + r % 4] = 1.0
+            one[a * 64 + r, (r // 4) * 8 + a * 4 + r % 4] = 1.0
+    return three, one
 
 
 def local(
@@ -465,7 +486,7 @@
         ],
         axis=1,
     )
-    q = jnp.asarray(rank_order(), bf16)
+    q, q8 = (jnp.asarray(v, bf16) for v in rank_orders())
 
     vm = pl.BlockSpec(memory_space=pltpu.VMEM)
     hbm = pl.BlockSpec(memory_space=pl.ANY)
@@ -478,7 +499,7 @@
             jax.ShapeDtypeStruct((2, 64, DS), f32),
             jax.ShapeDtypeStruct((2, 4, V), f32),
         ),
-        in_specs=[hbm, vm, hbm, hbm, vm, vm, vm, vm, vm],
+        in_specs=[hbm, vm, hbm, hbm, vm, vm, vm, vm, vm, vm],
         out_specs=(hbm, vm, vm, vm),
         scratch_shapes=[
             pltpu.VMEM((T, D), bf16),
@@ -486,10 +507,10 @@
             pltpu.VMEM((T, D), bf16),
             pltpu.VMEM((T, D), bf16),
             pltpu.VMEM((D, V), bf16),
-            pltpu.VMEM((NF, 2, A, DS), bf16),
-            pltpu.VMEM((16, V), f32),
-            pltpu.VMEM((16, V), bf16),
-            pltpu.VMEM((2 * A, V), bf16),
+            pltpu.VMEM((NF, 2, K3, DS), bf16),
+            pltpu.VMEM((32, V), f32),
+            pltpu.VMEM((32, V), bf16),
+            pltpu.VMEM((32 * NF, V), bf16),
             pltpu.VMEM((T, T + A), bf16),
             pltpu.VMEM((NF, A, DS), f32),
             pltpu.VMEM((4, 4, 64, DS), f32),
@@ -498,22 +519,22 @@
             pltpu.VMEM((4, 64, DS), f32),
             pltpu.VMEM((4, 64, DS), f32),
             pltpu.VMEM((4, 64, DS), f32),
-            pltpu.VMEM((2 * A, V), f32),
+            pltpu.VMEM((A, V), f32),
             pltpu.VMEM((NF, 8, V), f32),
             pltpu.VMEM((T, V + A), bf16),
             pltpu.VMEM((T, V + A), bf16),
-            pltpu.VMEM((T, 4 * A), bf16),
+            pltpu.VMEM((T, 4 * K3), bf16),
             pltpu.VMEM((2 * A, T), bf16),
-            pltpu.VMEM((2 * A, V), bf16),
+            pltpu.VMEM((2 * K3, V), bf16),
             pltpu.VMEM((T, V), f32),
-            pltpu.VMEM((T, 2 * A), f32),
+            pltpu.VMEM((T, A), f32),
             dma((G,)),
             dma((G,)),
             dma((G,)),
             dma((2,)),
-            dma((2,)),
+            dma((3,)),
             dma,
-            dma((4,)),
+            dma((5,)),
             dma,
             dma((NF, 2)),
             dma,
@@ -521,7 +542,7 @@
             dma((NF, 2)),
             dma,
             dma((NF,)),
-            dma((2,)),
+            dma((3,)),
             dma((G,)),
             dma((G,)),
             dma((4,)),
@@ -546,13 +567,24 @@
         selt,
         lab,
         q,
+        q8,
     )
-    return (
-        val.reshape(blocks, 8, V),
-        tg.reshape(blocks, 8, D),
-        dg,
-        ug,
-    )
+    pieces = [
+        pl.BlockSpec((blocks // 8, 8, D), lambda i: (i, 0, 0)),
+        pl.BlockSpec((blocks // 8, 8, V), lambda i: (i, 0, 0)),
+        pl.BlockSpec((2, 8, DS), lambda i: (0, i, 0)),
+        pl.BlockSpec((2, 4, V // 8), lambda i: (0, 0, i)),
+    ]
+    results = (tg.reshape(blocks, 8, D), val.reshape(blocks, 8, V), dg, ug)
+    tg, val, dg, ug = pl.pallas_call(
+        settle,
+        out_shape=tuple(jax.ShapeDtypeStruct(v.shape, v.dtype) for v in results),
+        grid=(8,),
+        in_specs=pieces,
+        out_specs=tuple(pieces),
+        name="settle",
+    )(*results)
+    return val, tg, dg, ug
 
 
 def solution(mesh):

time: 187 us -> 182 us (0.973)
  local copies, waits for them, and re-layouts: 8.46 us -> 0.59 us
  Pallas kernels: 174 us -> 176 us
    unnamed x8 -> x0, local copies, waits for them, and re-layouts: 7.87 us -> none
    pallas_call x0 -> x1, Pallas kernels: none -> 7.04 us  [local(): pl.pallas_call(settle, out_shape=tuple((jax.ShapeDtypeStruct(v.shape, v.d...]
    pallas_call x1, Pallas kernels: 174 us -> 169 us  [local(): pl.pallas_call(kernel, out_shape=(jax.ShapeDtypeStruct((T, D), bf16), jax...]
where the time goes in v4:
time: 182 us; the launch traced here: 180 us
  Pallas kernels  176 us (97%)
  other arithmetic  3.4 us (2%)
    pallas_call x1, Pallas kernels, local(): pl.pallas_call(kernel, out_shape=(jax.ShapeDtypeStruct((T, D), bf16), jax...  169 us
    pallas_call x1, Pallas kernels, local(): pl.pallas_call(settle, out_shape=tuple((jax.ShapeDtypeStruct(v.shape, v.d...  7.04 us

profile of v4, /device:TPU:1, one launch (start us, length us, event | category | flops | bytes accessed | tf_op | source)
XLA Modules:
  0.0 180.3 jit_solution(2894480708540498750)
XLA Ops:
  0.6 0.9 select_reduce_fusion.1
  1.5 0.7 multiply_subtract_fusion
  2.2 0.2 convert_reduce_fusion
  2.3 0.1 select_reduce_fusion.2
  2.5 0.1 broadcast_in_dim.38
  2.6 0.1 convert_element_type.25
  2.7 0.1 broadcast_in_dim.35
  2.7 0.1 mul.34
  2.8 0.1 broadcast_in_dim.32
  2.9 0.1 mul.32
  3.0 0.1 broadcast_in_dim.39
  3.1 0.1 fusion.2
  3.2 0.7 pad_maximum_fusion.lab
  3.9 0.8 fusion.1
  4.7 168.5 %lora_moves.1 = (bf16[256,8192]{1,0:T(8,128)(2,1)}, bf16[256,1024]{1,0:T(8,128)(2,1)}, f32[2,64,512]{2,1,0:T(8,128)}, f32[2,4,1024]{2,1,0:T(4,128)}) custom-call(bf16[256,8192]{1,0:T(8,128)(2,1)} %bitcast.6, bf16[256,1024]{1,0:T(8,128)(2,1)} %bitcast.7, bf16[512,1024]{1,0:T(8,128)(2,1)} %w.1, bf16[2,64,512]{2,1,0:T(8,128)(2,1)} %down.1, ...), custom_call_target="tpu_custom_call" | custom-call | flops 14000000000 | bytes 12582912 | tf_op jit(solution)/shard_map/lora_moves/pallas_call | solution.py:494
  173.2 7.0 %settle.1 = (bf16[32,8,8192]{2,1,0:T(8,128)(2,1)}, bf16[32,8,1024]{2,1,0:T(8,128)(2,1)}, f32[2,64,512]{2,1,0:T(8,128)}, f32[2,4,1024]{2,1,0:T(4,128)}) custom-call(bf16[32,8,8192]{2,1,0:T(8,128)(2,1)} %bitcast.4, bf16[32,8,1024]{2,1,0:T(8,128)(2,1)} %bitcast.5, f32[2,64,512]{2,1,0:T(8,128)} %get-tuple-element.14.dg, f32[2,4,1024]{2,1,0:T(4,128)} %get-tuple-element.15.ug), custom_call_target="tpu_custom_call" | custom-call | tf_op jit(solution)/shard_map/settle/pallas_call | solution.py:579
  (5 shorter events, 0.0 us)

commit v5 on v4

--- a/solution.py
+++ b/solution.py
@@ -325,12 +325,12 @@
 
     def arrived(g, _):
         done(xr.at[:, group(g)], x_recv.at[g])
+        down_terms(g)
 
         @pl.when(g + 1 < G)
         def _():
             grads_off(g + 1)
 
-        down_terms(g)
         return 0
 
     grads_off(0)
@@ -570,16 +570,16 @@
         q8,
     )
     pieces = [
-        pl.BlockSpec((blocks // 8, 8, D), lambda i: (i, 0, 0)),
-        pl.BlockSpec((blocks // 8, 8, V), lambda i: (i, 0, 0)),
-        pl.BlockSpec((2, 8, DS), lambda i: (0, i, 0)),
-        pl.BlockSpec((2, 4, V // 8), lambda i: (0, 0, i)),
+        pl.BlockSpec((blocks // 2, 8, D), lambda i: (i, 0, 0)),
+        pl.BlockSpec((blocks // 2, 8, V), lambda i: (i, 0, 0)),
+        pl.BlockSpec((2, 32, DS), lambda i: (0, i, 0)),
+        pl.BlockSpec((2, 4, V // 2), lambda i: (0, 0, i)),
     ]
     results = (tg.reshape(blocks, 8, D), val.reshape(blocks, 8, V), dg, ug)
     tg, val, dg, ug = pl.pallas_call(
         settle,
         out_shape=tuple(jax.ShapeDtypeStruct(v.shape, v.dtype) for v in results),
-        grid=(8,),
+        grid=(2,),
         in_specs=pieces,
         out_specs=tuple(pieces),
         name="settle",

time: 182 us -> 179 us (0.984)
  Pallas kernels: 176 us -> 172 us
    pallas_call x1, Pallas kernels: 7.04 us -> 4.05 us  [local(): pl.pallas_call(settle, out_shape=tuple((jax.ShapeDtypeStruct(v.shape, v.d...]
where the time goes in v5:
time: 179 us; the launch traced here: 177 us
  Pallas kernels  172 us (96%)
  other arithmetic  3.4 us (2%)
    pallas_call x1, Pallas kernels, local(): pl.pallas_call(kernel, out_shape=(jax.ShapeDtypeStruct((T, D), bf16), jax...  168 us
    pallas_call x1, Pallas kernels, local(): pl.pallas_call(settle, out_shape=tuple((jax.ShapeDtypeStruct(v.shape, v.d...  4.05 us

profile of v5, /device:TPU:1, one launch (start us, length us, event | category | flops | bytes accessed | tf_op | source)
XLA Modules:
  0.0 177.0 jit_solution(10166492103714833952)
XLA Ops:
  0.6 0.9 select_reduce_fusion.1
  1.5 0.7 multiply_subtract_fusion
  2.2 0.2 convert_reduce_fusion
  2.3 0.1 select_reduce_fusion.2
  2.5 0.1 broadcast_in_dim.38
  2.6 0.1 convert_element_type.25
  2.7 0.1 broadcast_in_dim.35
  2.7 0.1 mul.34
  2.8 0.1 broadcast_in_dim.32
  2.9 0.1 mul.32
  3.0 0.1 broadcast_in_dim.39
  3.1 0.1 fusion.2
  3.2 0.7 pad_maximum_fusion.lab
  3.9 0.8 fusion.1
  4.7 168.3 %lora_moves.1 = (bf16[256,8192]{1,0:T(8,128)(2,1)}, bf16[256,1024]{1,0:T(8,128)(2,1)}, f32[2,64,512]{2,1,0:T(8,128)}, f32[2,4,1024]{2,1,0:T(4,128)}) custom-call(bf16[256,8192]{1,0:T(8,128)(2,1)} %bitcast.6, bf16[256,1024]{1,0:T(8,128)(2,1)} %bitcast.7, bf16[512,1024]{1,0:T(8,128)(2,1)} %w.1, bf16[2,64,512]{2,1,0:T(8,128)(2,1)} %down.1, ...), custom_call_target="tpu_custom_call" | custom-call | flops 14000000000 | bytes 12582912 | tf_op jit(solution)/shard_map/lora_moves/pallas_call | solution.py:494
  173.0 4.0 %settle.1 = (bf16[32,8,8192]{2,1,0:T(8,128)(2,1)}, bf16[32,8,1024]{2,1,0:T(8,128)(2,1)}, f32[2,64,512]{2,1,0:T(8,128)}, f32[2,4,1024]{2,1,0:T(4,128)}) custom-call(bf16[32,8,8192]{2,1,0:T(8,128)(2,1)} %bitcast.4, bf16[32,8,1024]{2,1,0:T(8,128)(2,1)} %bitcast.5, f32[2,64,512]{2,1,0:T(8,128)} %get-tuple-element.14.dg, f32[2,4,1024]{2,1,0:T(4,128)} %get-tuple-element.15.ug), custom_call_target="tpu_custom_call" | custom-call | tf_op jit(solution)/shard_map/settle/pallas_call | solution.py:579
  (5 shorter events, 0.0 us)
